TPU v7x, 512 devices: a whole 4x8x8 slice. The times are simulated.
512 devices in a mesh: section: 2 (over core), seq: 64 (over y, z), mp: 4 (over x).
Axes of the slice: x: 4, y: 8, z: 8, core: 2. Of those that a mesh axis runs over, the one named last changes fastest.
Arguments:
- enc_rows: bfloat16 [2, 768, 1536], P('section', 'seq'), may hold values from -6 to 6
- vis_index: int32 [2, 768], P('section', 'seq'), may hold values from 0 to 8639, as said below
- owner_of: int32 [8640], replicated, may hold values from 0 to 63, as said below
- enc_gain: bfloat16 [1536], replicated, may hold values from 0.5 to 1.5
- embed_weight: bfloat16 [1536, 768], P('section'), may hold values from -0.15625 to 0.15625
- mask_token: bfloat16 [768], replicated, may hold values from -4 to 4
- attn_gain: bfloat16 [768], replicated, may hold values from 0.5 to 1.5
- qkv_weight: bfloat16 [768, 3, 768], P('section', None, 'mp')
- out_weight: bfloat16 [768, 768], P('mp', 'section'), may hold values from -0.21875 to 0.21875
- mlp_gain: bfloat16 [768], replicated, may hold values from 0.5 to 1.5
- up_weight: bfloat16 [768, 3072], P('section', 'mp'), may hold values from -0.21875 to 0.21875
- down_weight: bfloat16 [3072, 768], P('mp', 'section'), may hold values from -0.109375 to 0.109375
Outputs:
- decoded: float32 [2, 8640, 768], P('section', 'seq')
Inputs may be any that keep to these rules, and one draw needn't show every extreme that they name: `vis_index`: each volume's row names 768 different patches. `owner_of`: each owner owns exactly 135 patches.
All inputs are finite; a program needn't handle non-finite values.
Results may differ from a plain program's by a relative error of at most 0.012.
Values may be sent and summed in bfloat16 or wider, within the bound.
A program may use at most 64 MiB of HBM per device.

v0:
```python
import jax
import jax.numpy as jnp
from jax import lax
from jax.sharding import PartitionSpec as P

GX = 6
HD = 64


def place_codes(patches, features):
    half_width = features // 8
    coordinates = jnp.stack(
        [patches % GX, patches // GX % GX, patches // (GX * GX) % GX, patches // (GX * GX * GX)],
        axis=1,
    ).astype(jnp.float32)
    frequency = 1.0 / 10000.0 ** (jnp.arange(half_width, dtype=jnp.float32) / half_width)
    angles = coordinates[:, :, None] * frequency[None, None, :]
    return jnp.concatenate([jnp.sin(angles), jnp.cos(angles)], axis=2).reshape(
        patches.shape[0], features
    )


def layer_norm(values, scales):
    centred = values - jnp.mean(values, axis=-1, keepdims=True)
    spread = jnp.mean(centred * centred, axis=-1, keepdims=True)
    return centred * lax.rsqrt(spread + 1e-06) * scales.astype(jnp.float32)


def absorb(softmax_state, query_heads, key_rows, value_rows):
    peak_old, totals, context = softmax_state
    head_count = query_heads.shape[1]
    key_heads = key_rows.reshape(key_rows.shape[0], head_count, HD)
    value_heads = value_rows.reshape(value_rows.shape[0], head_count, HD)
    scores = jnp.einsum(
        "qhd,khd->hqk", query_heads, key_heads, preferred_element_type=jnp.float32
    ) * HD ** (-0.5)
    peak_new = jnp.maximum(peak_old, jnp.max(scores, axis=-1))
    factor = jnp.exp(peak_old - peak_new)
    exponent = jnp.exp(scores - peak_new[:, :, None])
    totals = totals * factor + jnp.sum(exponent, axis=-1)
    context = context * factor[:, :, None] + jnp.einsum(
        "hqk,khd->hqd",
        exponent.astype(jnp.bfloat16),
        value_heads,
        preferred_element_type=jnp.float32,
    )
    return (peak_new, totals, context)


def shards(
    enc_rows,
    vis_index,
    owner_of,
    enc_gain,
    embed_weight,
    mask_token,
    attn_gain,
    qkv_weight,
    out_weight,
    mlp_gain,
    up_weight,
    down_weight,
):
    normed_enc = layer_norm(enc_rows[0].astype(jnp.float32), enc_gain).astype(jnp.bfloat16)
    embed_full, qkv_full, out_full, up_full, down_full = (
        lax.all_gather(embed_weight, "section", axis=0, tiled=True),
        lax.all_gather(qkv_weight, "section", axis=0, tiled=True),
        lax.all_gather(out_weight, "section", axis=1, tiled=True),
        lax.all_gather(up_weight, "section", axis=0, tiled=True),
        lax.all_gather(down_weight, "section", axis=1, tiled=True),
    )
    embedded = jnp.dot(normed_enc, embed_full, preferred_element_type=jnp.float32).astype(
        jnp.bfloat16
    )
    features = qkv_full.shape[0]
    local_width = qkv_full.shape[2]
    head_count = local_width // HD
    patch_total = owner_of.shape[0]
    own_rows = patch_total // lax.axis_size("seq")
    owned_ids = jnp.nonzero(owner_of == lax.axis_index("seq"), size=own_rows)[0].astype(jnp.int32)
    own_codes = place_codes(owned_ids, features)
    mask_row = mask_token.astype(jnp.float32)
    visible_ids = vis_index[0]
    block_rows = GX * GX * GX * 4
    empty_state = (
        jnp.full((head_count, own_rows), -1e30, jnp.float32),
        jnp.zeros((head_count, own_rows), jnp.float32),
        jnp.zeros((head_count, own_rows, HD), jnp.float32),
    )
    all_rows, all_ids = (
        lax.all_gather(embedded, "seq", axis=0, tiled=True),
        lax.all_gather(visible_ids, "seq", axis=0, tiled=True),
    )
    matches = owned_ids[:, None] == all_ids[None, :]
    chosen = jnp.dot(matches.astype(jnp.bfloat16), all_rows, preferred_element_type=jnp.float32)
    stream = jnp.where(jnp.any(matches, axis=1)[:, None], chosen, mask_row[None, :]) + own_codes
    attn_in = layer_norm(stream, attn_gain).astype(jnp.bfloat16)
    projected = jnp.dot(
        attn_in, qkv_full.reshape(features, 3 * local_width), preferred_element_type=jnp.float32
    ).astype(jnp.bfloat16)
    query_heads = projected[:, :local_width].reshape(own_rows, head_count, HD)
    key_rows = projected[:, local_width : 2 * local_width]
    value_rows = projected[:, 2 * local_width :]
    state_now = empty_state
    key_piece = lax.all_gather(key_rows, "seq", axis=0, tiled=True)
    value_piece = lax.all_gather(value_rows, "seq", axis=0, tiled=True)
    row_count = key_piece.shape[0]
    for offset in range(0, row_count, block_rows):
        finish = min(offset + block_rows, row_count)
        state_now = absorb(
            state_now, query_heads, key_piece[offset:finish], value_piece[offset:finish]
        )
    peak_final, totals, context = state_now
    context = (
        jnp.transpose(context / totals[:, :, None], (1, 0, 2))
        .reshape(own_rows, local_width)
        .astype(jnp.bfloat16)
    )
    attn_part = jnp.dot(context, out_full, preferred_element_type=jnp.float32)
    middle = stream + lax.psum(attn_part.astype(jnp.bfloat16), "mp").astype(jnp.float32)
    mlp_in = layer_norm(middle, mlp_gain).astype(jnp.bfloat16)
    hidden = jax.nn.gelu(
        jnp.dot(mlp_in, up_full, preferred_element_type=jnp.float32), approximate=False
    ).astype(jnp.bfloat16)
    decoded = middle + lax.psum(
        jnp.dot(hidden, down_full, preferred_element_type=jnp.float32).astype(jnp.bfloat16), "mp"
    ).astype(jnp.float32)
    return decoded[None]


def solution(mesh):
    in_specs = (
        P("section", "seq", None),
        P("section", "seq"),
        P(),
        P(),
        P("section", None),
        P(),
        P(),
        P("section", None, "mp"),
        P("mp", "section"),
        P(),
        P("section", "mp"),
        P("mp", "section"),
    )
    out_specs = P("section", "seq", None)
    return jax.shard_map(shards, mesh=mesh, in_specs=in_specs, out_specs=out_specs, check_vma=False)
```

profile of v0, /device:TPU:8, one launch (start us, length us, event | category | flops | bytes accessed | tf_op | source)
XLA Modules:
  0.0 519.1 jit_solution(17662319799309199705)
XLA Ops:
  11.8 21.3 %all-gather.11.cloned.1.call-done = bf16[1536,768]{1,0:T(8,128)(2,1)} async-done(((bf16[768,768]{1,0:T(8,128)(2,1)}), bf16[1536,768]{1,0:T(8,128)(2,1)}) %all-gather.11.cloned.1.call-update) | async-done | bytes 2359312 | tf_op jit(solution)/shard_map/all_gather | solution.py:66
  33.1 2.7 fusion.42
  36.0 60.5 %scatter_custom_fusion = s32[135]{0:T(256)S(1)} fusion(s32[8640]{0:T(1024)S(1)} %compare_select_fusion, s32[8640]{0:T(1024)S(1)} %broadcast.227, s32[]{:T(128)} %constant.53.clone.1), kind=kCustom, calls=%fused_computation.240 | custom fusion | flops 8640 | bytes 544 | tf_op jit(solution)/shard_map/scatter-add | solution.py:80
  97.9 2.2 multiply_sine_fusion
  102.9 25.9 %all-reduce.2 = s32[768]{0:T(1024)S(1)} all-reduce(s32[768]{0:T(1024)S(1)} %bitcast_dynamic-update-slice_fusion), channel_id=2, replica_groups=mesh['section'=2,'seq'=64,'mp'=4] {'seq'}, use_global_device_ids=true, to_apply=%add.2 | all-reduce | flops 768 | bytes 6144
  129.0 2.4 all_gather.30
  131.5 2.2 reshape.534
  136.3 2.1 all_gather.33
  138.6 79.9 %all-gather.19.cloned.1.call-done = bf16[64,135,192]{2,1,0:T(8,128)(2,1)} async-done(((bf16[1,135,192]{2,1,0:T(8,128)(2,1)}), bf16[64,135,192]{2,1,0:T(8,128)(2,1)}) %all-gather.19.cloned.1.call-update) | async-done | bytes 3317776 | tf_op jit(solution)/shard_map/all_gather | solution.py:105
  218.5 7.5 %reshape.536 = bf16[8640,192]{1,0:T(8,128)(2,1)} reshape(bf16[64,135,192]{2,1,0:T(8,128)(2,1)} %all-gather.19.cloned.1.call-done) | data formatting | bytes 6635520
  226.0 3.6 fusion.179
  229.5 2.0 copy.96
  231.5 74.3 %all-gather.21.cloned.1.call-done = bf16[64,135,192]{2,1,0:T(8,128)(2,1)} async-done(((bf16[1,135,192]{2,1,0:T(8,128)(2,1)}), bf16[64,135,192]{2,1,0:T(8,128)(2,1)}) %all-gather.21.cloned.1.call-update) | async-done | bytes 3317776 | tf_op jit(solution)/shard_map/all_gather | solution.py:106
  305.8 7.5 %reshape.538 = bf16[8640,192]{1,0:T(8,128)(2,1)} reshape(bf16[64,135,192]{2,1,0:T(8,128)(2,1)} %all-gather.21.cloned.1.call-done) | data formatting | bytes 6635520
  313.3 4.3 fusion.178
  317.6 2.0 copy.111
  322.7 1.9 copy.105
  328.5 1.9 copy.99
  332.4 1.9 copy.95
  364.2 47.8 %all-reduce.6.cloned.1.call-done = bf16[135,768]{1,0:T(8,128)(2,1)} async-done(((bf16[135,768]{1,0:T(8,128)(2,1)}), bf16[135,768]{1,0:T(8,128)(2,1)}) %all-reduce.6.cloned.1.call-update) | async-done | bytes 207376 | tf_op jit(solution)/shard_map/psum | solution.py:120
  414.2 17.3 %all-gather.13.cloned.1.call-done = bf16[768,768]{1,0:T(8,128)(2,1)} async-done(((bf16[384,768]{1,0:T(8,128)(2,1)}), bf16[768,768]{1,0:T(8,128)(2,1)}) %all-gather.13.cloned.1.call-update) | async-done | bytes 1179664 | tf_op jit(solution)/shard_map/all_gather | solution.py:69
  431.6 21.0 %all-gather.15.cloned.1.call-done = bf16[768,768]{1,0:T(8,128)(2,1)} async-done(((bf16[768,384]{1,0:T(8,128)(2,1)}), bf16[768,768]{1,0:T(8,128)(2,1)}) %all-gather.15.cloned.1.call-update) | async-done | bytes 1179664 | tf_op jit(solution)/shard_map/all_gather | solution.py:70
  452.6 3.9 convolution_convert_fusion
  456.5 53.7 %all-reduce.8.cloned.1.call-done = bf16[135,768]{1,0:T(8,128)(2,1)} async-done(((bf16[135,768]{1,0:T(8,128)(2,1)}), bf16[135,768]{1,0:T(8,128)(2,1)}) %all-reduce.8.cloned.1.call-update) | async-done | bytes 207376 | tf_op jit(solution)/shard_map/psum | solution.py:125
  (150 shorter events, 54.5 us)
Async XLA Ops:
  6.5 4.8 copy-start.16
  6.5 26.6 %all-gather.11.cloned.1.call-start = ((), (), s32[]{:S(2)}) async-start(), calls=%async_computation | async-start | bytes 3538944 | tf_op jit(solution)/shard_map/all_gather | solution.py:66
  7.3 124.2 %all-gather.17.cloned.1.call-start = ((), (), s32[]{:S(2)}) async-start(), calls=%async_computation.5 | async-start | bytes 1597440 | tf_op jit(solution)/shard_map/all_gather | solution.py:91
  35.9 66.9 %copy-start.20 = (s32[1,12]{1,0:T(1,128)S(1)}, s32[1,12]{1,0:T(1,128)}, u32[]{:S(2)}) copy-start(s32[1,12]{1,0:T(1,128)} %param.13) | copy-start | bytes 148
  35.9 182.6 %all-gather.19.cloned.1.call-start = ((), (), s32[]{:S(2)}) async-start(), calls=%async_computation.6 | async-start | bytes 4526080 | tf_op jit(solution)/shard_map/all_gather | solution.py:105
  36.0 93.0 %copy-start.15 = (bf16[384,3,192]{0,2,1:T(8,128)(2,1)S(1)}, bf16[384,3,192]{0,2,1:T(8,128)(2,1)}, u32[]{:S(2)}) copy-start(bf16[384,3,192]{0,2,1:T(8,128)(2,1)} %param.19) | copy-start | bytes 1327108
  134.2 2.1 copy-start.18
  135.7 170.1 %all-gather.21.cloned.1.call-start = ((), (), s32[]{:S(2)}) async-start(), calls=%async_computation.7 | async-start | bytes 4526080 | tf_op jit(solution)/shard_map/all_gather | solution.py:106
  136.3 275.8 %all-reduce.6.cloned.1.call-start = ((), (), s32[]{:S(2)}) async-start(), calls=%async_computation.1 | async-start | bytes 417792 | tf_op jit(solution)/shard_map/psum | solution.py:120
  345.7 1.1 copy-start.13
  346.2 1.1 copy-start.12
  346.8 1.1 copy-start.11
  347.3 1.1 copy-start.10
  347.9 1.1 copy-start.8
  353.9 1.2 copy-start.7
  355.6 1.0 copy-start.5
  356.6 1.0 copy-start.4
  357.2 1.0 copy-start.3
  358.8 1.0 copy-start.1
  361.8 2.3 copy-start.19
  362.8 68.8 %all-gather.13.cloned.1.call-start = ((), (), s32[]{:S(2)}) async-start(), calls=%async_computation.2 | async-start | bytes 1769472 | tf_op jit(solution)/shard_map/all_gather | solution.py:69
  363.4 89.2 %all-gather.15.cloned.1.call-start = ((), (), s32[]{:S(2)}) async-start(), calls=%async_computation.3 | async-start | bytes 1769472 | tf_op jit(solution)/shard_map/all_gather | solution.py:70
  364.1 146.0 %all-reduce.8.cloned.1.call-start = ((), (), s32[]{:S(2)}) async-start(), calls=%async_computation.4 | async-start | bytes 417792 | tf_op jit(solution)/shard_map/psum | solution.py:125
  414.2 95.9 %copy-start = (bf16[135,768]{1,0:T(8,128)(2,1)S(1)}, bf16[135,768]{1,0:T(8,128)(2,1)}, u32[]{:S(2)}) copy-start(bf16[135,768]{1,0:T(8,128)(2,1)} %all-reduce.6.cloned.1.call-done) | copy-start | bytes 622084
  (5 other events, 4.9 us)
Sparse Core Ops, SparseCore 0:
  9.4 23.6 all-gather.10
  36.2 83.7 all-gather.16
  135.8 82.6 all-gather.18
  221.4 84.3 all-gather.20
  362.9 49.0 all-reduce.5
  414.2 17.3 all-gather.12
  433.9 18.6 all-gather.14
  456.6 53.4 all-reduce.7
where the time goes:
time: 521 us; the launch traced here: 519 us
  waiting for transfers between devices  318 us (61%)
  other arithmetic  76.9 us (15%)
  local copies, waits for them, and re-layouts  59.6 us (11%)
  blocking collectives  30.5 us (6%)
  matrix products  19.3 us (4%)
  between operations  14.6 us (3%)
    all_gather x1, waiting for transfers between devices, shards(): key_piece = lax.all_gather(key_rows, 'seq', axis=0, tiled=True)  79.9 us
    all_gather x1, waiting for transfers between devices, shards(): value_piece = lax.all_gather(value_rows, 'seq', axis=0, tiled=True)  74.3 us
    scatter-add x1, other arithmetic, shards(): jnp.nonzero(owner_of == lax.axis_index('seq'), size=own_rows)[0]  60.5 us
    psum x1, waiting for transfers between devices, shards(): lax.psum(jnp.dot(hidden, down_full, preferred_element_type=jnp.float32).a...  53.7 us
    psum x1, waiting for transfers between devices, shards(): lax.psum(attn_part.astype(jnp.bfloat16), 'mp').astype(jnp.float32)  47.8 us
    unnamed x1, blocking collectives  25.9 us
    slice x11, local copies, waits for them, and re-layouts, shards(): value_piece[offset:finish]  22.9 us
    all_gather x1, waiting for transfers between devices, shards(): lax.all_gather(embed_weight, 'section', axis=0, tiled=True)  21.3 us
  transfers between devices with their start and end apart: 8, of which 7 were waited for; matrix products, arithmetic and copies ran while one was open for 17% of the time, Pallas kernels for 0%

commit v1 on v0

v1 whole, which is shorter than its diff:
```python
import functools

import jax
import jax.numpy as jnp
import numpy as np
from jax import lax
from jax.experimental import pallas as pl
from jax.experimental.pallas import tpu as pltpu
from jax.sharding import PartitionSpec as P

MESH = pl.DeviceIdType.MESH
F32 = jnp.float32
BF16 = jnp.bfloat16
GX = 6
PATCHES = 8640
OWN = 135
ROWS = 144
VIS_DEV = 12
WIDTH = 768
ENC = 1536
LOCAL = 192
HD = 64
NEG = -1e30
KEYS = 8704
CHUNK = 2176


def code_table():
    half = WIDTH // 8
    frequency = (1.0 / 10000.0 ** (np.arange(half, dtype=np.float32) / half)).astype(np.float32)
    table = np.zeros((64, WIDTH), np.float32)
    for c, (base, count) in enumerate(((0, GX), (8, GX), (16, GX), (24, 40))):
        angle = np.arange(count, dtype=np.float32)[:, None] * frequency[None, :]
        table[base : base + count, c * 192 : c * 192 + half] = np.sin(angle)
        table[base : base + count, c * 192 + half : (c + 1) * 192] = np.cos(angle)
    pieces = []
    for _ in range(3):
        piece = table.astype(BF16)
        pieces.append(piece)
        table = table - piece.astype(np.float32)
    return np.concatenate(pieces, axis=0)


def iota(shape, axis):
    return lax.broadcasted_iota(jnp.int32, shape, axis)


def fiota(shape, axis):
    return iota(shape, axis).astype(F32)


def nn(a, b):
    return lax.dot_general(a, b, (((1,), (0,)), ((), ())), preferred_element_type=F32)


def nt(a, b):
    return lax.dot_general(a, b, (((1,), (1,)), ((), ())), preferred_element_type=F32)


def coordinates(patch):
    c3 = jnp.floor((patch + 0.5) * (1.0 / 216.0))
    rest = patch - 216.0 * c3
    c2 = jnp.floor((rest + 0.5) * (1.0 / 36.0))
    rest = rest - 36.0 * c2
    c1 = jnp.floor((rest + 0.5) * (1.0 / 6.0))
    return rest - 6.0 * c1, c1, c2, c3


def one_hot_rows(patch, lanes):
    c0, c1, c2, c3 = coordinates(patch)
    lane = (iota((patch.shape[0], lanes), 1) & 63).astype(F32)
    value = jnp.where(
        lane < 8, c0, jnp.where(lane < 16, c1 + 8, jnp.where(lane < 24, c2 + 16, c3 + 24))
    )
    return jnp.where(lane == value, 1.0, 0.0).astype(BF16)


def norm(values):
    centred = values - jnp.mean(values, axis=-1, keepdims=True)
    spread = jnp.mean(centred * centred, axis=-1, keepdims=True)
    return centred * lax.rsqrt(spread + 1e-06)


def select(target, source, count):
    lane = fiota((target.shape[0], count), 1)
    return jnp.where(lane == source, 1.0, 0.0).astype(BF16)


def kernel(
    enc, vis, owner, vecs, ct3, embed_w, qkv_w, out_w, up_w, down_w,
    result,
    E2, W2, O2, U2, D2, encf, vrow, P1, P2, R1, R2, GQ, GE, GK1, GK2, IDG,
    rankf, KT, VT, XC, XE, PB, RX, YX, SC, QB, ACC, MX, LS, STREAM, MID,
    loc_sem, ws, wr, os_, or_, fs, fr, p1s, p1r, p2s, p2r,
    ids_s, ids_r, qs, qr, es, er, k1s, k1r, k2s, k2r,
    xcs, xcr, xes, xer, rss, rsr, ags, agr,
):
    s = lax.axis_index("section")
    seq = lax.axis_index("seq")
    m = lax.axis_index("mp")
    y = seq // 8
    z = seq % 8
    partner = {"section": 1 - s}

    def zdev(k):
        return {"seq": y * 8 + (z + k) % 8}

    def ydev(k):
        return {"seq": ((y + k) % 8) * 8 + z}

    def xdev(k):
        return {"mp": (m + k) % 4}

    def remote(src, dst, send, recv, device):
        return pltpu.make_async_remote_copy(
            src_ref=src, dst_ref=dst, send_sem=send, recv_sem=recv, device_id=device, device_id_type=MESH
        )

    def ring(n, first=1):
        def run(f):
            lax.fori_loop(first, n, lambda k, c: (f(k), c)[1], 0)

        return run

    def halves(ref_out, ref_in, i):
        return pltpu.make_async_copy(ref_in, ref_out.at[s], loc_sem.at[i])

    barrier = pltpu.get_barrier_semaphore()
    pl.semaphore_signal(barrier, inc=1, device_id=partner, device_id_type=MESH)
    ring(8)(lambda k: pl.semaphore_signal(barrier, inc=1, device_id=zdev(k), device_id_type=MESH))
    ring(8)(lambda k: pl.semaphore_signal(barrier, inc=1, device_id=ydev(k), device_id_type=MESH))
    ring(4)(lambda k: pl.semaphore_signal(barrier, inc=1, device_id=xdev(k), device_id_type=MESH))

    own_out = pltpu.make_async_copy(out_w, O2.at[s, m, pl.ds(0, LOCAL)], loc_sem.at[4])
    local = [halves(E2, embed_w, 0), halves(W2, qkv_w, 1), halves(U2, up_w, 2), halves(D2, down_w, 3), own_out]
    for copy in local:
        copy.start()
    pad = jnp.zeros((64, 384), BF16)
    for i in range(4):
        O2[s, i, LOCAL:256, :] = pad
    pl.semaphore_wait(barrier, 18)

    weights = [
        remote(src, dst.at[s], ws.at[i], wr.at[i], partner)
        for i, (src, dst) in enumerate(((embed_w, E2), (qkv_w, W2), (up_w, U2), (down_w, D2)))
    ]
    weights[0].start()
    weights[1].start()

    def out_copy(k):
        return remote(out_w, O2.at[s, m, pl.ds(0, LOCAL)], os_.at[k], or_.at[k], xdev(k))

    ring(4)(lambda k: out_copy(k).start())

    mask_row = vecs[0:1, :]
    attn_gain = vecs[1:2, :]
    mlp_gain = vecs[2:3, :]
    enc_gain = jnp.concatenate([vecs[3:4, :], vecs[4:5, :]], axis=1)
    table = ct3[...]
    vrow[...] = jnp.full((8, 128), -1.0, F32)
    vrow[0:1, 0:VIS_DEV] = vis[...].astype(F32)
    vids = vrow[0:1, :]
    vcol = jnp.sum(
        jnp.where(iota((16, 128), 1) == iota((16, 128), 0), jnp.broadcast_to(vids, (16, 128)), 0.0),
        axis=1, keepdims=True,
    )
    vis_code = nn(one_hot_rows(jnp.maximum(vcol, 0.0), 192), table)
    encf[...] = jnp.zeros((16, ENC), F32)
    encf[0:VIS_DEV, :] = enc[0].astype(F32)
    normed = (norm(encf[...]) * enc_gain).astype(BF16)

    flags = jnp.where(owner[...] == seq, 1.0, 0.0).astype(F32)
    flagb = flags.astype(BF16)
    upper = jnp.where(iota((128, 128), 0) <= iota((128, 128), 1), 1.0, 0.0).astype(BF16)
    lower = jnp.where(iota((72, 72), 1) < iota((72, 72), 0), 1.0, 0.0).astype(BF16)
    within = nn(flagb, upper)
    before = jnp.sum(nn(lower, flagb), axis=1, keepdims=True)
    rankf[...] = jnp.where(flags > 0.5, within + before - 1.0, -1.0)
    own_j = fiota((ROWS, 128), 0)
    lane_row = fiota((ROWS, 128), 1)

    def find(h, total):
        row = jnp.broadcast_to(rankf[pl.ds(h, 1), :], (ROWS, 128))
        return total + jnp.where(row == own_j, lane_row + (h * 128).astype(F32), 0.0)

    own_ids = jnp.sum(
        lax.fori_loop(0, 68, find, jnp.zeros((ROWS, 128), F32), unroll=4), axis=1, keepdims=True
    )
    own_code = nn(one_hot_rows(own_ids, 192), table)

    row64 = iota((64, WIDTH), 0)
    lane64 = iota((64, WIDTH), 1)
    group = jnp.where(row64 < 8, 0, jnp.where(row64 < 16, 1, jnp.where(row64 < 24, 2, 3)))
    inside = (lane64 >= group * 192) & (lane64 < group * 192 + 192)
    mask_centred = mask_row - jnp.mean(mask_row, axis=-1, keepdims=True)
    code = table[0:64].astype(F32) + table[64:128].astype(F32) + table[128:192].astype(F32)
    block = jnp.where(inside, mask_centred + code, 0.0)
    block_sum = jnp.sum(block, axis=1, keepdims=True)
    block_mean = block_sum * (1.0 / 192.0)
    off = jnp.where(inside, block - block_mean, 0.0)
    spread = jnp.sum(off * off, axis=1, keepdims=True)
    scaled = (block - block_sum * (1.0 / 768.0)) * attn_gain
    scaled_hi = scaled.astype(BF16)
    scaled_lo = (scaled - scaled_hi.astype(F32)).astype(BF16)
    pieces = jnp.concatenate([scaled_hi, scaled_lo], axis=0)
    lane128 = iota((64, 128), 1)
    row128 = iota((64, 128), 0)
    group128 = jnp.where(row128 < 8, 0, jnp.where(row128 < 16, 1, jnp.where(row128 < 24, 2, 3)))
    stat = jnp.where(lane128 == group128, block_mean, 0.0) + jnp.where(lane128 == 4, spread, 0.0)
    stat_t = jnp.transpose(jnp.concatenate([stat, stat], axis=0))[0:16, :]

    local[0].wait()
    weights[0].wait_recv()
    embedded = (nn(normed[:, 0:WIDTH], E2[0]) + nn(normed[:, WIDTH:ENC], E2[1])).astype(BF16)
    attn_vis = (norm(embedded.astype(F32) + vis_code) * attn_gain).astype(BF16)
    local[1].wait()
    weights[1].wait_recv()
    qk = nt(attn_vis[:, 0:384], W2[0, 0:384, :]) + nt(attn_vis[:, 384:768], W2[1, 0:384, :])
    kv = nt(attn_vis[:, 0:384], W2[0, LOCAL:576, :]) + nt(attn_vis[:, 384:768], W2[1, LOCAL:576, :])
    lane16 = iota((16, 384), 1)
    row16 = fiota((16, 1), 0)

    def pick(low, high, shift):
        return select(row16, jnp.where((row16 >= low) & (row16 < high), row16 + shift, -1.0), 16)

    first, second, third = pick(0, 6, 0), pick(0, 6, 6), pick(6, 12, -6)

    def pack(pair, keys_values):
        left = jnp.where(lane16 < LOCAL, pair, 0.0).astype(BF16)
        right = jnp.where(lane16 >= LOCAL, pltpu.roll(pair, LOCAL, 1), 0.0).astype(BF16)
        return nn(first, left) + nn(second, right) + nn(keys_values, kv.astype(BF16))

    vhi = jnp.floor((vids + 0.5) * (1.0 / 128.0))
    vlo = vids - 128.0 * vhi
    row_ids = iota((16, 128), 0)
    id_part = jnp.where(row_ids == 12, vhi, jnp.where(row_ids == 13, vlo, 0.0))
    id_part = jnp.concatenate([id_part, jnp.zeros((16, 256), F32)], axis=1)
    P1[...] = (pack(qk, third) + id_part).astype(BF16)
    quarter = pltpu.roll(embedded.astype(F32), (WIDTH - m * LOCAL) % WIDTH, 1)[:, 0:384]
    P2[...] = pack(quarter, pick(6, 12, 0)).astype(BF16)
    R1[z] = P1[...]
    R2[y] = P2[...]

    def p1_copy(k):
        return remote(P1, R1.at[z], p1s.at[k], p1r.at[k], zdev(k))

    def p2_copy(k):
        return remote(P2, R2.at[y], p2s.at[k], p2r.at[k], ydev(k))

    ring(8)(lambda k: (p1_copy(k).start(), p2_copy(k).start()))
    weights[2].start()
    weights[3].start()

    kv_w0, kv_w1 = W2[0, LOCAL:576, :], W2[1, LOCAL:576, :]
    proj = nt(kv_w0, pieces[:, 0:384]) + nt(kv_w1, pieces[:, 384:768])
    proj = proj + pltpu.roll(proj, 64, 1)
    proj_hi = proj.astype(BF16)
    lane_p = iota((384, 128), 1)
    kv_table = jnp.where(lane_p < 64, proj_hi.astype(F32), proj - proj_hi.astype(F32)).astype(BF16)
    stat_hi = stat_t.astype(BF16)
    stat_table = jnp.where(
        iota((16, 128), 1) < 64, stat_hi.astype(F32), stat_t - stat_hi.astype(F32)
    ).astype(BF16)
    big_table = jnp.concatenate([kv_table, stat_table], axis=0)

    stream0 = mask_row + own_code
    attn_own = (norm(stream0) * attn_gain).astype(BF16)
    q_masked = nt(attn_own[:, 0:384], W2[0, 0:256, :]) + nt(attn_own[:, 384:768], W2[1, 0:256, :])

    def build(c):
        width = 512
        start = pl.multiple_of(c * width, width)
        patch = (iota((1, width), 1) + start).astype(F32)
        c0, c1, c2, c3 = coordinates(patch)
        sub = fiota((64, width), 0)
        value = jnp.where(
            sub < 8, c0, jnp.where(sub < 16, c1 + 8, jnp.where(sub < 24, c2 + 16, c3 + 24))
        )
        hot = jnp.where(sub == value, 1.0, 0.0).astype(BF16)
        raw = nn(big_table, jnp.concatenate([hot, hot], axis=0))
        m0, m1, m2, m3 = raw[384:385], raw[385:386], raw[386:387], raw[387:388]
        mean = (m0 + m1 + m2 + m3) * 0.25
        between = (m0 - mean) ** 2 + (m1 - mean) ** 2 + (m2 - mean) ** 2 + (m3 - mean) ** 2
        scale = lax.rsqrt(raw[388:389] * (1.0 / 768.0) + between * 0.25 + 1e-06)
        KT[0:LOCAL, pl.ds(start, width)] = (raw[0:LOCAL] * scale).astype(BF16)
        VT[0:LOCAL, pl.ds(start, width)] = (raw[LOCAL:384] * scale).astype(BF16)
        KT[LOCAL:256, pl.ds(start, width)] = jnp.zeros((64, width), BF16)
        VT[LOCAL:256, pl.ds(start, width)] = jnp.zeros((64, width), BF16)

    lax.fori_loop(0, 6, lambda c, x: (build(c), x)[1], 0)

    def wait_in(copies, n, slot, ref, sem):
        def one(k, c):
            remote(ref.at[slot(k)], ref.at[slot(k)], sem.at[k], sem.at[k], partner).wait_recv()
            return c

        lax.fori_loop(1, n, one, 0)

    def from_z(k):
        return (z + 8 - k) % 8

    def from_y(k):
        return (y + 8 - k) % 8

    def from_x(k):
        return (m + 4 - k) % 4

    wait_in(None, 8, from_z, R1, p1r)
    wait_in(None, 8, from_y, R2, p2r)
    col = fiota((112, 1), 0)
    small = jnp.where(col < 48, col, col - 48)
    src = jnp.floor((small + 0.5) * (1.0 / 6.0))
    src = 16.0 * src + (small - 6.0 * src) + jnp.where(col < 48, 0.0, 6.0)
    src = jnp.where(col < 96, src, jnp.where(col < 104, 16.0 * (col - 96) + 12, 16.0 * (col - 104) + 13))
    chooser = select(col, src, 128)
    got1 = nn(chooser, R1[...].reshape(128, 384))
    got2 = nn(chooser[0:96], R2[...].reshape(128, 384))
    GQ[y] = got1[0:48].astype(BF16)
    GK1[y] = got1[48:96].astype(BF16)
    IDG[y] = 128.0 * got1[96:104, 0:128] + got1[104:112, 0:128]
    GE[z] = got2[0:48].astype(BF16)
    GK2[z] = got2[48:96].astype(BF16)

    def over(ref, slot, send, recv, device):
        def copy(k):
            return remote(ref.at[slot], ref.at[slot], send.at[k], recv.at[k], device(k))

        return copy

    c_ids = over(IDG, y, ids_s, ids_r, ydev)
    c_q = over(GQ, y, qs, qr, ydev)
    c_e = over(GE, z, es, er, zdev)
    c_k1 = over(GK1, y, k1s, k1r, ydev)
    c_k2 = over(GK2, z, k2s, k2r, zdev)
    ring(8)(lambda k: (c_ids(k).start(), c_q(k).start(), c_e(k).start()))
    ring(8)(lambda k: (c_k1(k).start(), c_k2(k).start()))

    local[4].wait()
    wait_in(None, 4, lambda k: (s, from_x(k), pl.ds(0, LOCAL)), O2, or_)
    forward = remote(O2.at[s], O2.at[s], fs.at[0], fr.at[0], partner)
    forward.start()

    lax.fori_loop(6, 17, lambda c, x: (build(c), x)[1], 0)

    wait_in(None, 8, from_y, IDG, ids_r)
    ids = IDG[...].reshape(64, 128)
    lane_i = fiota((64, 128), 1)
    source = fiota((64, 1), 0) + 1.0
    hots, where_d, where_i = [], [], []
    for i in range(VIS_DEV):
        one = ids[:, i : i + 1]
        high = jnp.floor((one + 0.5) * (1.0 / 128.0))
        low = one - 128.0 * high
        hots.append(jnp.where(lane_i == high, 1.0, 0.0))
        hot = jnp.where(lane_i == low, 1.0, 0.0)
        where_d.append((hot * source).astype(BF16))
        where_i.append((hot * float(i)).astype(BF16))
    hot_t = jnp.transpose(jnp.concatenate(hots, axis=0)).astype(BF16)
    found = nn(
        hot_t,
        jnp.concatenate(
            [jnp.concatenate(where_d, axis=0), jnp.concatenate(where_i, axis=0)], axis=1
        ),
    )
    seen = found[:, 0:128]
    patch2 = fiota((128, 128), 0) * 128.0 + fiota((128, 128), 1)
    bias = jnp.where((seen > 0.5) | (patch2 >= PATCHES), NEG, 0.0)
    sub16 = iota((16, 128), 0)
    for h in range(68):
        KT[LOCAL : LOCAL + 16, h * 128 : (h + 1) * 128] = jnp.where(
            sub16 == 0, jnp.broadcast_to(bias[h : h + 1, :], (16, 128)), 0.0
        ).astype(BF16)
    own_hi = jnp.floor((own_ids + 0.5) * (1.0 / 128.0))
    own_lo = own_ids - 128.0 * own_hi
    hit_hi = jnp.where(lane_row == own_hi, 1.0, 0.0).astype(BF16)
    hit_lo = lane_row == own_lo
    place = nn(hit_hi, found.astype(BF16))
    own_d = jnp.sum(jnp.where(hit_lo, place[:, 0:128], 0.0), axis=1, keepdims=True) - 1.0
    own_i = jnp.sum(jnp.where(hit_lo, place[:, 128:256], 0.0), axis=1, keepdims=True)
    is_vis = own_d > -0.5
    late = own_i > 5.5
    own_i6 = jnp.where(late, own_i - 6.0, own_i)
    own_y = jnp.floor((own_d + 0.5) * 0.125)
    own_z = own_d - 8.0 * own_y
    row_yz = own_y * 48.0 + own_z * 6.0 + own_i6
    row_zy = own_z * 48.0 + own_y * 6.0 + own_i6

    def choose(row, gathered):
        lane = fiota((ROWS, 384), 1)
        hit = jnp.where((lane == row) & is_vis, 1.0, 0.0)
        one = nn(jnp.where(late, 0.0, hit).astype(BF16), gathered)
        two = nn(jnp.where(late, hit, 0.0).astype(BF16), gathered)
        both = one + pltpu.roll(two, LOCAL, 1)
        return jnp.where(iota((ROWS, 256), 1) < LOCAL, both[:, 0:256], 0.0)

    wait_in(None, 8, from_y, GQ, qr)
    q_vis = choose(row_yz, GQ[...].reshape(384, 384))
    queries = jnp.where(is_vis, q_vis, q_masked).astype(BF16).astype(F32) * (HD ** -0.5)
    lane_q = iota((ROWS, 256), 1)
    for h in range(3):
        keep = (lane_q >= h * HD) & (lane_q < (h + 1) * HD)
        QB[h * ROWS : (h + 1) * ROWS, :] = jnp.where(
            keep, queries, jnp.where(lane_q == LOCAL, 1.0, 0.0)
        ).astype(BF16)

    wait_in(None, 8, from_z, GE, er)
    XE[m] = choose(row_zy, GE[...].reshape(384, 384)).astype(BF16)

    c_xe = over(XE, m, xes, xer, xdev)
    ring(4)(lambda k: c_xe(k).start())

    MX[...] = jnp.full((3 * ROWS, 128), NEG, F32)
    LS[...] = jnp.zeros((3 * ROWS, 128), F32)
    ACC[...] = jnp.zeros((3 * ROWS, 256), F32)

    def absorb(scores, width, product):
        peak_old = MX[...]
        peak = jnp.maximum(peak_old, jnp.max(scores, axis=1, keepdims=True))
        factor = jnp.exp(peak_old - peak)
        weights_ = jnp.exp(scores - peak[:, 0:1])
        total = weights_[:, 0:128]
        for t in range(1, width // 128):
            total = total + weights_[:, t * 128 : (t + 1) * 128]
        MX[...] = peak
        LS[...] = LS[...] * factor + total
        ACC[...] = ACC[...] * jnp.concatenate([factor, factor], axis=1) + product(weights_.astype(BF16))

    def masked(c, x):
        start = pl.multiple_of(c * CHUNK, 128)
        scores = nn(QB[...], KT[:, pl.ds(start, CHUNK)])
        absorb(scores, CHUNK, lambda w: nt(w, VT[:, pl.ds(start, CHUNK)]))
        return x

    lax.fori_loop(0, KEYS // CHUNK, masked, 0)

    wait_in(None, 8, from_y, GK1, k1r)
    wait_in(None, 8, from_z, GK2, k2r)
    q_only = jnp.where(iota((3 * ROWS, 256), 1) < LOCAL, QB[...].astype(F32), 0.0).astype(BF16)

    def visible(gathered):
        scores = nt(q_only, gathered[:, 0:256])
        absorb(scores, 384, lambda w: pltpu.roll(nn(w, gathered), LOCAL, 1)[:, 0:256])

    visible(GK1[...].reshape(384, 384))
    visible(GK2[...].reshape(384, 384))

    context = jnp.zeros((ROWS, 256), F32)
    for h in range(3):
        keep = (lane_q >= h * HD) & (lane_q < (h + 1) * HD)
        part = slice(h * ROWS, (h + 1) * ROWS)
        total = jnp.sum(LS[part, :], axis=1, keepdims=True)
        context = context + jnp.where(keep, ACC[part, :] / total, 0.0)
    XC[m] = context.astype(BF16)
    c_xc = over(XC, m, xcs, xcr, xdev)
    ring(4)(lambda k: c_xc(k).start())

    wait_in(None, 4, from_x, XE, xer)
    filled = jnp.zeros((ROWS, WIDTH), F32)
    for i in range(4):
        wide = jnp.concatenate([XE[i].astype(F32), jnp.zeros((ROWS, 512), F32)], axis=1)
        filled = filled + (pltpu.roll(wide, i * LOCAL, 1) if i else wide)
    stream = jnp.where(is_vis, filled, mask_row) + own_code
    STREAM[...] = stream

    local[2].wait()
    local[3].wait()
    weights[2].wait_recv()
    weights[3].wait_recv()
    forward.wait_recv()
    wait_in(None, 4, from_x, XC, xcr)
    gathered = jnp.concatenate([XC[i] for i in range(4)], axis=1)
    for half in range(2):
        cols = slice(half * 384, (half + 1) * 384)
        MID[:, cols] = STREAM[:, cols] + nn(gathered, O2[half].reshape(1024, 384))

    mlp_in = (norm(MID[...]) * mlp_gain).astype(BF16)
    raised = nn(mlp_in[:, 0:384], U2[0]) + nn(mlp_in[:, 384:768], U2[1])
    hidden = (0.5 * raised * (1.0 + lax.erf(raised * np.float32(np.sqrt(0.5))))).astype(BF16)
    for half in range(2):
        PB[half] = nn(hidden, D2[half]).astype(BF16)

    def quadrant(q):
        return PB.at[q % 2, pl.ds(pl.multiple_of((q // 2) * 64, 16), 80)]

    def rs_copy(k):
        return remote(quadrant((m + k) % 4), RX.at[m], rss.at[k], rsr.at[k], xdev(k))

    ring(4)(lambda k: rs_copy(k).start())
    RX[m] = PB[m % 2, pl.ds(pl.multiple_of((m // 2) * 64, 16), 80), :]
    wait_in(None, 4, from_x, RX, rsr)
    YX[m] = (
        RX[0].astype(F32) + RX[1].astype(F32) + RX[2].astype(F32) + RX[3].astype(F32)
    ).astype(BF16)
    c_ag = over(YX, m, ags, agr, xdev)
    ring(4)(lambda k: c_ag(k).start())
    wait_in(None, 4, from_x, YX, agr)
    for half in range(2):
        cols = slice(half * 384, (half + 1) * 384)
        result[0:80, cols] = MID[0:80, cols] + YX[half].astype(F32)
        result[80:OWN, cols] = MID[80:OWN, cols] + YX[2 + half].astype(F32)[16:71]

    for copy in weights:
        copy.wait_send()
    forward.wait_send()
    ring(4)(lambda k: (out_copy(k).wait_send(), c_xe(k).wait_send(), c_xc(k).wait_send()))
    ring(4)(lambda k: (rs_copy(k).wait_send(), c_ag(k).wait_send()))
    ring(8)(lambda k: (p1_copy(k).wait_send(), p2_copy(k).wait_send(), c_ids(k).wait_send()))
    ring(8)(lambda k: (c_q(k).wait_send(), c_e(k).wait_send(), c_k1(k).wait_send(), c_k2(k).wait_send()))


def shards(
    enc_rows, vis_index, owner_of, enc_gain, embed_weight, mask_token, attn_gain, qkv_weight,
    out_weight, mlp_gain, up_weight, down_weight,
):
    owner = jnp.pad(owner_of, (0, 72 * 128 - PATCHES), constant_values=-1).reshape(72, 128)
    vecs = jnp.stack(
        [mask_token, attn_gain, mlp_gain, enc_gain[:WIDTH], enc_gain[WIDTH:]], axis=0
    ).astype(F32)
    qkv_t = jnp.transpose(qkv_weight, (1, 2, 0)).reshape(576, 384)
    vm = pl.BlockSpec(memory_space=pltpu.VMEM)
    hbm = pl.BlockSpec(memory_space=pl.ANY)
    dma = pltpu.SemaphoreType.DMA
    V = pltpu.VMEM
    scratch = [
        V((2, 768, 768), BF16), V((2, 576, 384), BF16), V((2, 4, 256, 384), BF16),
        V((2, 384, 768), BF16), V((2, 768, 384), BF16),
        V((16, ENC), F32), V((8, 128), F32), V((16, 384), BF16), V((16, 384), BF16),
        V((8, 16, 384), BF16), V((8, 16, 384), BF16),
        V((8, 48, 384), BF16), V((8, 48, 384), BF16), V((8, 48, 384), BF16), V((8, 48, 384), BF16),
        V((8, 8, 128), F32), V((72, 128), F32),
        V((256, KEYS), BF16), V((256, KEYS), BF16),
        V((4, ROWS, 256), BF16), V((4, ROWS, 256), BF16),
        V((2, ROWS, 384), BF16), V((4, 80, 384), BF16), V((4, 80, 384), BF16),
        V((8, 128), F32), V((3 * ROWS, 256), BF16), V((3 * ROWS, 256), F32),
        V((3 * ROWS, 128), F32), V((3 * ROWS, 128), F32), V((ROWS, WIDTH), F32), V((ROWS, WIDTH), F32),
        dma((5,)), dma((4,)), dma((4,)), dma((4,)), dma((4,)), dma((1,)), dma((1,)),
    ] + [dma((8,))] * 14 + [dma((4,))] * 8
    decoded = pl.pallas_call(
        kernel,
        out_shape=jax.ShapeDtypeStruct((OWN, WIDTH), F32),
        in_specs=[vm, vm, vm, vm, vm, hbm, hbm, hbm, hbm, hbm],
        out_specs=vm,
        scratch_shapes=scratch,
        compiler_params=pltpu.CompilerParams(
            collective_id=0, has_side_effects=True, vmem_limit_bytes=56 * 1024 * 1024
        ),
        cost_estimate=pl.CostEstimate(flops=6_000_000_000, bytes_accessed=5_000_000, transcendentals=4_000_000),
    )(enc_rows, vis_index, owner, vecs, jnp.asarray(code_table()), embed_weight, qkv_t, out_weight, up_weight, down_weight)
    return decoded[None]


def solution(mesh):
    in_specs = (
        P("section", "seq", None),
        P("section", "seq"),
        P(),
        P(),
        P("section", None),
        P(),
        P(),
        P("section", None, "mp"),
        P("mp", "section"),
        P(),
        P("section", "mp"),
        P("mp", "section"),
    )
    out_specs = P("section", "seq", None)
    return jax.shard_map(shards, mesh=mesh, in_specs=in_specs, out_specs=out_specs, check_vma=False)
```

time: 521 us -> 74.4 us (0.14)
  the two profiles are of different devices: /device:TPU:8 before, /device:TPU:64 now
where the time goes in v1:
time: 74.4 us; the launch traced here: 74.1 us
  Pallas kernels  67 us (90%)
  local copies, waits for them, and re-layouts  6.43 us (9%)
    pallas_call x1, Pallas kernels, shards(): pl.pallas_call(kernel, out_shape=jax.ShapeDtypeStruct((OWN, WIDTH), F32),...  67 us
    broadcast_in_dim x1, local copies, waits for them, and re-layouts, shards(): return decoded[None]  2.18 us
    another operation x6, local copies, waits for them, and re-layouts, shards(): jnp.stack([mask_token, attn_gain, mlp_gain, enc_gain[:WIDTH], enc_gain[WI...  2.1 us

profile of v1, /device:TPU:64, one launch (start us, length us, event | category | flops | bytes accessed | tf_op | source)
XLA Modules:
  0.0 74.1 jit_solution(10935663794895942499)
XLA Ops:
  0.0 0.7 stack.18
  0.7 0.7 stack.19
  1.4 0.7 stack.20
  2.1 0.8 %fusion = (bf16[768]{0:T(1024)(128)(2,1)S(1)}, bf16[768]{0:T(1024)(128)(2,1)S(1)}) fusion(bf16[1536]{0:T(1024)(128)(2,1)} %param.16), kind=kLoop, calls=%fused_computation.1 | loop fusion | bytes 6144 | tf_op jit(solution)/shard_map/slice | solution.py:517
  2.9 0.6 convert_element_type.3.vecs
  3.5 1.4 %pad_bitcast_fusion.owner = s32[72,128]{1,0:T(8,128)} fusion(s32[8640]{0:T(1024)} %param.15), kind=kLoop, calls=%fused_computation | loop fusion | bytes 71424 | tf_op jit(solution)/shard_map/reshape | solution.py:515
  4.9 67.0 %shard_map.127 = f32[135,768]{1,0:T(8,128)} custom-call(bf16[1,12,1536]{2,1,0:T(8,128)(2,1)} %enc.1, s32[1,12]{1,0:T(1,128)} %vis.1, s32[72,128]{1,0:T(8,128)} %pad_bitcast_fusion.owner, f32[5,768]{1,0:T(8,128)} %convert_element_type.3.vecs, bf16[192,768]{1,0:T(8,128)(2,1)} %constant.4.clone.ct3, bf16[768,768]{1,0:T(8,128)(2,1)} %embed_w.1, ...), custom_call_target="tpu_custom_call" | custom-call | flops 6000000000 | bytes 5000000 | tf_op jit(solution)/shard_map/pallas_call | solution.py:538
  71.9 2.2 %copy.14 = f32[1,135,768]{2,0,1:T(1,128)} copy(f32[1,135,768]{2,1,0:T(8,128)} %bitcast.6) | data formatting | bytes 829440 | tf_op jit(solution)/shard_map/broadcast_in_dim | solution.py:549
  (3 shorter events, 0.0 us)

commit v2 on v1

--- a/solution.py
+++ b/solution.py
@@ -87,12 +87,13 @@
 
 
 def kernel(
-    enc, vis, owner, vecs, ct3, embed_w, qkv_w, out_w, up_w, down_w,
+    enc, vis, owner, enc_g, mask_t, attn_g, mlp_g, ct3, embed_w, qkv_w, out_w, up_w, down_w,
     result,
-    E2, W2, O2, U2, D2, encf, vrow, P1, P2, R1, R2, GQ, GE, GK1, GK2, IDG,
+    E2, W2, OA, OB, U2, D2, own2, encf, vrow, P1, P2, R1, R2, GQ, GE, GK1, GK2, IDG,
     rankf, KT, VT, XC, XE, PB, RX, YX, SC, QB, ACC, MX, LS, STREAM, MID,
-    loc_sem, ws, wr, os_, or_, fs, fr, p1s, p1r, p2s, p2r,
-    ids_s, ids_r, qs, qr, es, er, k1s, k1r, k2s, k2r,
+    loc_sem, ws, wr, os_, or_, os2, or2, fs, fr, p1s, p1r, p2s, p2r,
+    ids_ps, ids_pr, ids_ms, ids_mr, q_ps, q_pr, q_ms, q_mr, e_ps, e_pr, e_ms, e_mr,
+    k1_ps, k1_pr, k1_ms, k1_mr, k2_ps, k2_pr, k2_ms, k2_mr,
     xcs, xcr, xes, xer, rss, rsr, ags, agr,
 ):
     s = lax.axis_index("section")
@@ -122,6 +123,113 @@
 
         return run
 
+    groups = []
+
+    class Group:
+        def __init__(self, copy, n, slot, ref, recv):
+            self.copy, self.n, self.slot, self.ref, self.sem = copy, n, slot, ref, recv
+            self.waited = False
+            groups.append(self)
+            ring(n)(lambda k: copy(k).start())
+
+        def wait_one(self, k):
+            there = self.ref.at[self.slot(k)]
+            remote(there, there, self.sem.at[k], self.sem.at[k], partner).wait_recv()
+
+        def wait(self):
+            self.waited = True
+            ring(self.n)(self.wait_one)
+
+        def left(self):
+            ring(self.n)(lambda k: self.copy(k).wait_send())
+
+    class Single:
+        def __init__(self, copy):
+            self.copy = copy
+            self.waited = False
+            groups.append(self)
+            copy.start()
+
+        def wait(self):
+            self.waited = True
+            self.copy.wait_recv()
+
+        def left(self):
+            self.copy.wait_send()
+
+    class Ring:
+        def __init__(self, ref, me, device, plus, sems):
+            self.ref, self.me, self.device, self.plus, self.minus = ref, me, device, plus, 7 - plus
+            self.ps, self.pr, self.ms, self.mr = sems
+            self.waited = False
+            groups.append(self)
+            self.up(1).start()
+            self.down(1).start()
+
+        def up(self, t):
+            block = self.ref.at[(self.me + 9 - t) % 8]
+            return remote(block, block, self.ps.at[t], self.pr.at[t], self.device(1))
+
+        def down(self, t):
+            block = self.ref.at[(self.me + t - 1) % 8]
+            return remote(block, block, self.ms.at[t], self.mr.at[t], self.device(7))
+
+        def hop(self, t):
+            def receive(block, sem):
+                there = self.ref.at[block]
+                remote(there, there, sem.at[t], sem.at[t], partner).wait_recv()
+
+            def guard(condition, f):
+                if isinstance(t, int):
+                    if condition:
+                        f()
+                else:
+                    pl.when(condition)(f)
+
+            guard(t <= self.plus, lambda: receive((self.me + 8 - t) % 8, self.pr))
+            guard(t < self.plus, lambda: self.up(t + 1).start())
+            guard(t <= self.minus, lambda: receive((self.me + t) % 8, self.mr))
+            guard(t < self.minus, lambda: self.down(t + 1).start())
+            if isinstance(t, int) and t == 4:
+                self.waited = True
+
+        def wait(self):
+            for t in range(1, 5):
+                self.hop(t)
+
+        def left(self):
+            ring(self.plus + 1)(lambda t: self.up(t).wait_send())
+            ring(self.minus + 1)(lambda t: self.down(t).wait_send())
+
+    class Local:
+        def __init__(self, copy):
+            self.copy = copy
+            self.waited = False
+            groups.append(self)
+            copy.start()
+
+        def wait(self):
+            self.waited = True
+            self.copy.wait()
+
+        def left(self):
+            pass
+
+    def finish():
+        for g in groups:
+            if not g.waited:
+                g.wait()
+            g.left()
+
+    def from_z(k):
+        return (z + 8 - k) % 8
+
+    def from_y(k):
+        return (y + 8 - k) % 8
+
+    def from_x(k):
+        return (m + 4 - k) % 4
+
     def halves(ref_out, ref_in, i):
         return pltpu.make_async_copy(ref_in, ref_out.at[s], loc_sem.at[i])
 
@@ -131,31 +239,21 @@
     ring(8)(lambda k: pl.semaphore_signal(barrier, inc=1, device_id=ydev(k), device_id_type=MESH))
     ring(4)(lambda k: pl.semaphore_signal(barrier, inc=1, device_id=xdev(k), device_id_type=MESH))
 
-    own_out = pltpu.make_async_copy(out_w, O2.at[s, m, pl.ds(0, LOCAL)], loc_sem.at[4])
-    local = [halves(E2, embed_w, 0), halves(W2, qkv_w, 1), halves(U2, up_w, 2), halves(D2, down_w, 3), own_out]
-    for copy in local:
-        copy.start()
-    pad = jnp.zeros((64, 384), BF16)
-    for i in range(4):
-        O2[s, i, LOCAL:256, :] = pad
-    pl.semaphore_wait(barrier, 18)
-
-    weights = [
-        remote(src, dst.at[s], ws.at[i], wr.at[i], partner)
-        for i, (src, dst) in enumerate(((embed_w, E2), (qkv_w, W2), (up_w, U2), (down_w, D2)))
+    local = [
+        Local(copy)
+        for copy in (
+            halves(E2, embed_w, 0), halves(W2, qkv_w, 1), halves(U2, up_w, 2), halves(D2, down_w, 3),
+            pltpu.make_async_copy(out_w.at[pl.ds(HD, 128)], OA.at[s, m], loc_sem.at[4]),
+            pltpu.make_async_copy(out_w.at[pl.ds(0, HD)], OB.at[s, m], loc_sem.at[5]),
+        )
     ]
-    weights[0].start()
-    weights[1].start()
-
-    def out_copy(k):
-        return remote(out_w, O2.at[s, m, pl.ds(0, LOCAL)], os_.at[k], or_.at[k], xdev(k))
-
-    ring(4)(lambda k: out_copy(k).start())
-
-    mask_row = vecs[0:1, :]
-    attn_gain = vecs[1:2, :]
-    mlp_gain = vecs[2:3, :]
-    enc_gain = jnp.concatenate([vecs[3:4, :], vecs[4:5, :]], axis=1)
+
+    mask_row = mask_t[...].astype(F32).reshape(1, WIDTH)
+    attn_gain = attn_g[...].astype(F32).reshape(1, WIDTH)
+    mlp_gain = mlp_g[...].astype(F32).reshape(1, WIDTH)
+    enc_gain = jnp.concatenate(
+        [enc_g[0:WIDTH].astype(F32).reshape(1, WIDTH), enc_g[WIDTH:ENC].astype(F32).reshape(1, WIDTH)], axis=1
+    )
     table = ct3[...]
     vrow[...] = jnp.full((8, 128), -1.0, F32)
     vrow[0:1, 0:VIS_DEV] = vis[...].astype(F32)
@@ -169,7 +267,13 @@
     encf[0:VIS_DEV, :] = enc[0].astype(F32)
     normed = (norm(encf[...]) * enc_gain).astype(BF16)
 
-    flags = jnp.where(owner[...] == seq, 1.0, 0.0).astype(F32)
+    own2[...] = jnp.full((72, 128), -1, jnp.int32)
+    for i in range(8):
+        own2[i * 8 : (i + 1) * 8, :] = owner[i * 1024 : (i + 1) * 1024].reshape(8, 128)
+    for i in range(64, 67):
+        own2[i : i + 1, :] = owner[i * 128 : (i + 1) * 128].reshape(1, 128)
+    own2[67:68, 0:64] = owner[67 * 128 : PATCHES].reshape(1, 64)
+    flags = jnp.where(own2[...] == seq, 1.0, 0.0).astype(F32)
     flagb = flags.astype(BF16)
     upper = jnp.where(iota((128, 128), 0) <= iota((128, 128), 1), 1.0, 0.0).astype(BF16)
     lower = jnp.where(iota((72, 72), 1) < iota((72, 72), 0), 1.0, 0.0).astype(BF16)
@@ -186,6 +290,22 @@
     own_ids = jnp.sum(
         lax.fori_loop(0, 68, find, jnp.zeros((ROWS, 128), F32), unroll=4), axis=1, keepdims=True
     )
+    pl.semaphore_wait(barrier, 18)
+
+    def weight(i, src, dst):
+        return Single(remote(src, dst.at[s], ws.at[i], wr.at[i], partner))
+
+    g_embed = weight(0, embed_w, E2)
+    g_qkv = weight(1, qkv_w, W2)
+
+    def oa_copy(k):
+        return remote(out_w.at[pl.ds(HD, 128)], OA.at[s, m], os_.at[k], or_.at[k], xdev(k))
+
+    def ob_copy(k):
+        return remote(out_w.at[pl.ds(0, HD)], OB.at[s, m], os2.at[k], or2.at[k], xdev(k))
+
+    g_oa = Group(oa_copy, 4, lambda k: (s, from_x(k)), OA, or_)
+    g_ob = Group(ob_copy, 4, lambda k: (s, from_x(k)), OB, or2)
     own_code = nn(one_hot_rows(own_ids, 192), table)
 
     row64 = iota((64, WIDTH), 0)
@@ -210,11 +330,11 @@
     stat_t = jnp.transpose(jnp.concatenate([stat, stat], axis=0))[0:16, :]
 
     local[0].wait()
-    weights[0].wait_recv()
+    g_embed.wait()
     embedded = (nn(normed[:, 0:WIDTH], E2[0]) + nn(normed[:, WIDTH:ENC], E2[1])).astype(BF16)
     attn_vis = (norm(embedded.astype(F32) + vis_code) * attn_gain).astype(BF16)
     local[1].wait()
-    weights[1].wait_recv()
+    g_qkv.wait()
     qk = nt(attn_vis[:, 0:384], W2[0, 0:384, :]) + nt(attn_vis[:, 384:768], W2[1, 0:384, :])
     kv = nt(attn_vis[:, 0:384], W2[0, LOCAL:576, :]) + nt(attn_vis[:, 384:768], W2[1, LOCAL:576, :])
     lane16 = iota((16, 384), 1)
@@ -247,9 +367,10 @@
     def p2_copy(k):
         return remote(P2, R2.at[y], p2s.at[k], p2r.at[k], ydev(k))
 
-    ring(8)(lambda k: (p1_copy(k).start(), p2_copy(k).start()))
-    weights[2].start()
-    weights[3].start()
+    g_p1 = Group(p1_copy, 8, from_z, R1, p1r)
+    g_p2 = Group(p2_copy, 8, from_y, R2, p2r)
+    g_up = weight(2, up_w, U2)
+    g_down = weight(3, down_w, D2)
 
     kv_w0, kv_w1 = W2[0, LOCAL:576, :], W2[1, LOCAL:576, :]
     proj = nt(kv_w0, pieces[:, 0:384]) + nt(kv_w1, pieces[:, 384:768])
@@ -283,30 +404,14 @@
         between = (m0 - mean) ** 2 + (m1 - mean) ** 2 + (m2 - mean) ** 2 + (m3 - mean) ** 2
         scale = lax.rsqrt(raw[388:389] * (1.0 / 768.0) + between * 0.25 + 1e-06)
         KT[0:LOCAL, pl.ds(start, width)] = (raw[0:LOCAL] * scale).astype(BF16)
-        VT[0:LOCAL, pl.ds(start, width)] = (raw[LOCAL:384] * scale).astype(BF16)
+        VT[HD:256, pl.ds(start, width)] = (raw[LOCAL:384] * scale).astype(BF16)
         KT[LOCAL:256, pl.ds(start, width)] = jnp.zeros((64, width), BF16)
-        VT[LOCAL:256, pl.ds(start, width)] = jnp.zeros((64, width), BF16)
+        VT[0:HD, pl.ds(start, width)] = jnp.zeros((64, width), BF16)
 
     lax.fori_loop(0, 6, lambda c, x: (build(c), x)[1], 0)
 
-    def wait_in(copies, n, slot, ref, sem):
-        def one(k, c):
-            remote(ref.at[slot(k)], ref.at[slot(k)], sem.at[k], sem.at[k], partner).wait_recv()
-            return c
-
-        lax.fori_loop(1, n, one, 0)
-
-    def from_z(k):
-        return (z + 8 - k) % 8
-
-    def from_y(k):
-        return (y + 8 - k) % 8
-
-    def from_x(k):
-        return (m + 4 - k) % 4
-
-    wait_in(None, 8, from_z, R1, p1r)
-    wait_in(None, 8, from_y, R2, p2r)
+    g_p1.wait()
+    g_p2.wait()
     col = fiota((112, 1), 0)
     small = jnp.where(col < 48, col, col - 48)
     src = jnp.floor((small + 0.5) * (1.0 / 6.0))
@@ -321,28 +426,41 @@
     GE[z] = got2[0:48].astype(BF16)
     GK2[z] = got2[48:96].astype(BF16)
 
-    def over(ref, slot, send, recv, device):
+    def over(n, ref, slot, source, send, recv, device):
         def copy(k):
             return remote(ref.at[slot], ref.at[slot], send.at[k], recv.at[k], device(k))
 
-        return copy
-
-    c_ids = over(IDG, y, ids_s, ids_r, ydev)
-    c_q = over(GQ, y, qs, qr, ydev)
-    c_e = over(GE, z, es, er, zdev)
-    c_k1 = over(GK1, y, k1s, k1r, ydev)
-    c_k2 = over(GK2, z, k2s, k2r, zdev)
-    ring(8)(lambda k: (c_ids(k).start(), c_q(k).start(), c_e(k).start()))
-    ring(8)(lambda k: (c_k1(k).start(), c_k2(k).start()))
-
+        return Group(copy, n, source, ref, recv)
+
+    r_ids = Ring(IDG, y, ydev, 4, (ids_ps, ids_pr, ids_ms, ids_mr))
+    r_q = Ring(GQ, y, ydev, 4, (q_ps, q_pr, q_ms, q_mr))
+    r_e = Ring(GE, z, zdev, 4, (e_ps, e_pr, e_ms, e_mr))
+
+    def build_some(low, high):
+        lax.fori_loop(low, high, lambda c, x: (build(c), x)[1], 0)
+
+    def hop_early(t):
+        r_ids.hop(t)
+        r_q.hop(t)
+        r_e.hop(t)
+
+    build_some(6, 9)
+    hop_early(1)
     local[4].wait()
-    wait_in(None, 4, lambda k: (s, from_x(k), pl.ds(0, LOCAL)), O2, or_)
-    forward = remote(O2.at[s], O2.at[s], fs.at[0], fr.at[0], partner)
-    forward.start()
-
-    lax.fori_loop(6, 17, lambda c, x: (build(c), x)[1], 0)
-
-    wait_in(None, 8, from_y, IDG, ids_r)
+    local[5].wait()
+    g_oa.wait()
+    g_ob.wait()
+    forward_a = Single(remote(OA.at[s], OA.at[s], fs.at[0], fr.at[0], partner))
+    forward_b = Single(remote(OB.at[s], OB.at[s], fs.at[1], fr.at[1], partner))
+    build_some(9, 12)
+    hop_early(2)
+    build_some(12, 15)
+    hop_early(3)
+    r_k1 = Ring(GK1, y, ydev, 3, (k1_ps, k1_pr, k1_ms, k1_mr))
+    r_k2 = Ring(GK2, z, zdev, 3, (k2_ps, k2_pr, k2_ms, k2_mr))
+    build_some(15, 17)
+    hop_early(4)
+
     ids = IDG[...].reshape(64, 128)
     lane_i = fiota((64, 128), 1)
     source = fiota((64, 1), 0) + 1.0
@@ -393,7 +511,6 @@
         both = one + pltpu.roll(two, LOCAL, 1)
         return jnp.where(iota((ROWS, 256), 1) < LOCAL, both[:, 0:256], 0.0)
 
-    wait_in(None, 8, from_y, GQ, qr)
     q_vis = choose(row_yz, GQ[...].reshape(384, 384))
     queries = jnp.where(is_vis, q_vis, q_masked).astype(BF16).astype(F32) * (HD ** -0.5)
     lane_q = iota((ROWS, 256), 1)
@@ -403,11 +520,9 @@
             keep, queries, jnp.where(lane_q == LOCAL, 1.0, 0.0)
         ).astype(BF16)
 
-    wait_in(None, 8, from_z, GE, er)
     XE[m] = choose(row_zy, GE[...].reshape(384, 384)).astype(BF16)
 
-    c_xe = over(XE, m, xes, xer, xdev)
-    ring(4)(lambda k: c_xe(k).start())
+    c_xe = over(4, XE, m, from_x, xes, xer, xdev)
 
     MX[...] = jnp.full((3 * ROWS, 128), NEG, F32)
     LS[...] = jnp.zeros((3 * ROWS, 128), F32)
@@ -426,35 +541,34 @@
         ACC[...] = ACC[...] * jnp.concatenate([factor, factor], axis=1) + product(weights_.astype(BF16))
 
     def masked(c, x):
+        r_k1.hop(c + 1)
+        r_k2.hop(c + 1)
         start = pl.multiple_of(c * CHUNK, 128)
         scores = nn(QB[...], KT[:, pl.ds(start, CHUNK)])
         absorb(scores, CHUNK, lambda w: nt(w, VT[:, pl.ds(start, CHUNK)]))
         return x
 
     lax.fori_loop(0, KEYS // CHUNK, masked, 0)
-
-    wait_in(None, 8, from_y, GK1, k1r)
-    wait_in(None, 8, from_z, GK2, k2r)
+    r_k1.waited = r_k2.waited = True
+
     q_only = jnp.where(iota((3 * ROWS, 256), 1) < LOCAL, QB[...].astype(F32), 0.0).astype(BF16)
 
-    def visible(gathered):
-        scores = nt(q_only, gathered[:, 0:256])
-        absorb(scores, 384, lambda w: pltpu.roll(nn(w, gathered), LOCAL, 1)[:, 0:256])
-
-    visible(GK1[...].reshape(384, 384))
-    visible(GK2[...].reshape(384, 384))
+    seen_rows = jnp.concatenate([GK1[...].reshape(384, 384), GK2[...].reshape(384, 384)], axis=0)
+    absorb(nt(q_only, seen_rows[:, 0:256]), 768, lambda w: nn(w, seen_rows[:, 128:384]))
 
     context = jnp.zeros((ROWS, 256), F32)
     for h in range(3):
-        keep = (lane_q >= h * HD) & (lane_q < (h + 1) * HD)
+        keep = (lane_q >= (h + 1) * HD) & (lane_q < (h + 2) * HD)
         part = slice(h * ROWS, (h + 1) * ROWS)
         total = jnp.sum(LS[part, :], axis=1, keepdims=True)
         context = context + jnp.where(keep, ACC[part, :] / total, 0.0)
-    XC[m] = context.astype(BF16)
-    c_xc = over(XC, m, xcs, xcr, xdev)
-    ring(4)(lambda k: c_xc(k).start())
-
-    wait_in(None, 4, from_x, XE, xer)
+    head0 = context[:, 0:128]
+    lane80 = iota((80, 128), 1)
+    XC[m, 0:ROWS, :] = context[:, 128:256].astype(BF16)
+    XC[m, ROWS:224, :] = jnp.where(lane80 < HD, pltpu.roll(head0[0:80], HD, 1), head0[64:ROWS]).astype(BF16)
+    c_xc = over(4, XC, m, from_x, xcs, xcr, xdev)
+
+    c_xe.wait()
     filled = jnp.zeros((ROWS, WIDTH), F32)
     for i in range(4):
         wide = jnp.concatenate([XE[i].astype(F32), jnp.zeros((ROWS, 512), F32)], axis=1)
@@ -464,14 +578,26 @@
 
     local[2].wait()
     local[3].wait()
-    weights[2].wait_recv()
-    weights[3].wait_recv()
-    forward.wait_recv()
-    wait_in(None, 4, from_x, XC, xcr)
-    gathered = jnp.concatenate([XC[i] for i in range(4)], axis=1)
+    g_up.wait()
+    g_down.wait()
+    forward_a.wait()
+    forward_b.wait()
+    c_xc.wait()
+    pairs = jnp.concatenate([XC[i, 0:ROWS, :] for i in range(4)], axis=1)
+    lows, highs = [], []
+    for i in (0, 2):
+        one, two = XC[i, ROWS:224, :].astype(F32), XC[i + 1, ROWS:224, :].astype(F32)
+        lows.append(jnp.where(lane80 < HD, one, pltpu.roll(two, HD, 1)).astype(BF16))
+        highs.append(jnp.where(lane80 < HD, pltpu.roll(one, HD, 1), two).astype(BF16))
+    singles = jnp.concatenate(
+        [jnp.concatenate(lows, axis=1), jnp.concatenate(highs, axis=1)], axis=0
+    )
     for half in range(2):
         cols = slice(half * 384, (half + 1) * 384)
-        MID[:, cols] = STREAM[:, cols] + nn(gathered, O2[half].reshape(1024, 384))
+        most = STREAM[:, cols] + nn(pairs, OA[half].reshape(512, 384))
+        rest = nn(singles, OB[half].reshape(256, 384))
+        MID[0:80, cols] = most[0:80] + rest[0:80]
+        MID[80:ROWS, cols] = most[80:ROWS] + rest[96:160]
 
     mlp_in = (norm(MID[...]) * mlp_gain).astype(BF16)
     raised = nn(mlp_in[:, 0:384], U2[0]) + nn(mlp_in[:, 384:768], U2[1])
@@ -485,68 +611,60 @@
     def rs_copy(k):
         return remote(quadrant((m + k) % 4), RX.at[m], rss.at[k], rsr.at[k], xdev(k))
 
-    ring(4)(lambda k: rs_copy(k).start())
+    c_rs = Group(rs_copy, 4, from_x, RX, rsr)
     RX[m] = PB[m % 2, pl.ds(pl.multiple_of((m // 2) * 64, 16), 80), :]
-    wait_in(None, 4, from_x, RX, rsr)
+    c_rs.wait()
     YX[m] = (
         RX[0].astype(F32) + RX[1].astype(F32) + RX[2].astype(F32) + RX[3].astype(F32)
     ).astype(BF16)
-    c_ag = over(YX, m, ags, agr, xdev)
-    ring(4)(lambda k: c_ag(k).start())
-    wait_in(None, 4, from_x, YX, agr)
+    c_ag = over(4, YX, m, from_x, ags, agr, xdev)
+    c_ag.wait()
     for half in range(2):
         cols = slice(half * 384, (half + 1) * 384)
-        result[0:80, cols] = MID[0:80, cols] + YX[half].astype(F32)
-        result[80:OWN, cols] = MID[80:OWN, cols] + YX[2 + half].astype(F32)[16:71]
-
-    for copy in weights:
-        copy.wait_send()
-    forward.wait_send()
-    ring(4)(lambda k: (out_copy(k).wait_send(), c_xe(k).wait_send(), c_xc(k).wait_send()))
-    ring(4)(lambda k: (rs_copy(k).wait_send(), c_ag(k).wait_send()))
-    ring(8)(lambda k: (p1_copy(k).wait_send(), p2_copy(k).wait_send(), c_ids(k).wait_send()))
-    ring(8)(lambda k: (c_q(k).wait_send(), c_e(k).wait_send(), c_k1(k).wait_send(), c_k2(k).wait_send()))
+        result[0:80, :, cols] = (MID[0:80, cols] + YX[half].astype(F32))[:, None, :]
+        result[80:OWN, :, cols] = (MID[80:OWN, cols] + YX[2 + half].astype(F32)[16:71])[:, None, :]
+
+    finish()
 
 
 def shards(
     enc_rows, vis_index, owner_of, enc_gain, embed_weight, mask_token, attn_gain, qkv_weight,
     out_weight, mlp_gain, up_weight, down_weight,
 ):
-    owner = jnp.pad(owner_of, (0, 72 * 128 - PATCHES), constant_values=-1).reshape(72, 128)
-    vecs = jnp.stack(
-        [mask_token, attn_gain, mlp_gain, enc_gain[:WIDTH], enc_gain[WIDTH:]], axis=0
-    ).astype(F32)
     qkv_t = jnp.transpose(qkv_weight, (1, 2, 0)).reshape(576, 384)
     vm = pl.BlockSpec(memory_space=pltpu.VMEM)
     hbm = pl.BlockSpec(memory_space=pl.ANY)
     dma = pltpu.SemaphoreType.DMA
     V = pltpu.VMEM
     scratch = [
-        V((2, 768, 768), BF16), V((2, 576, 384), BF16), V((2, 4, 256, 384), BF16),
-        V((2, 384, 768), BF16), V((2, 768, 384), BF16),
+        V((2, 768, 768), BF16), V((2, 576, 384), BF16), V((2, 4, 128, 384), BF16), V((2, 4, 64, 384), BF16),
+        V((2, 384, 768), BF16), V((2, 768, 384), BF16), V((72, 128), jnp.int32),
         V((16, ENC), F32), V((8, 128), F32), V((16, 384), BF16), V((16, 384), BF16),
         V((8, 16, 384), BF16), V((8, 16, 384), BF16),
         V((8, 48, 384), BF16), V((8, 48, 384), BF16), V((8, 48, 384), BF16), V((8, 48, 384), BF16),
         V((8, 8, 128), F32), V((72, 128), F32),
         V((256, KEYS), BF16), V((256, KEYS), BF16),
-        V((4, ROWS, 256), BF16), V((4, ROWS, 256), BF16),
+        V((4, 224, 128), BF16), V((4, ROWS, 256), BF16),
         V((2, ROWS, 384), BF16), V((4, 80, 384), BF16), V((4, 80, 384), BF16),
         V((8, 128), F32), V((3 * ROWS, 256), BF16), V((3 * ROWS, 256), F32),
         V((3 * ROWS, 128), F32), V((3 * ROWS, 128), F32), V((ROWS, WIDTH), F32), V((ROWS, WIDTH), F32),
-        dma((5,)), dma((4,)), dma((4,)), dma((4,)), dma((4,)), dma((1,)), dma((1,)),
-    ] + [dma((8,))] * 14 + [dma((4,))] * 8
+        dma((6,)), dma((4,)), dma((4,)), dma((4,)), dma((4,)), dma((4,)), dma((4,)), dma((2,)), dma((2,)),
+    ] + [dma((8,))] * 4 + [dma((5,))] * 20 + [dma((4,))] * 8
     decoded = pl.pallas_call(
         kernel,
-        out_shape=jax.ShapeDtypeStruct((OWN, WIDTH), F32),
-        in_specs=[vm, vm, vm, vm, vm, hbm, hbm, hbm, hbm, hbm],
+        out_shape=jax.ShapeDtypeStruct((OWN, 1, WIDTH), F32),
+        in_specs=[vm] * 8 + [hbm, hbm, hbm, hbm, hbm],
         out_specs=vm,
         scratch_shapes=scratch,
         compiler_params=pltpu.CompilerParams(
             collective_id=0, has_side_effects=True, vmem_limit_bytes=56 * 1024 * 1024
         ),
         cost_estimate=pl.CostEstimate(flops=6_000_000_000, bytes_accessed=5_000_000, transcendentals=4_000_000),
-    )(enc_rows, vis_index, owner, vecs, jnp.asarray(code_table()), embed_weight, qkv_t, out_weight, up_weight, down_weight)
-    return decoded[None]
+    )(
+        enc_rows, vis_index, owner_of, enc_gain, mask_token, attn_gain, mlp_gain, jnp.asarray(code_table()),
+        embed_weight, qkv_t, out_weight, up_weight, down_weight,
+    )
+    return jnp.transpose(decoded, (1, 0, 2))
 
 
 def solution(mesh):

time: 74.4 us -> 74.8 us (level)
  the two profiles are of different devices: /device:TPU:64 before, /device:TPU:8 now
where the time goes in v2:
time: 74.8 us; the launch traced here: 74.5 us
  Pallas kernels  72.5 us (97%)
  local copies, waits for them, and re-layouts  2.04 us (3%)
    pallas_call x1, Pallas kernels, shards(): pl.pallas_call(kernel, out_shape=jax.ShapeDtypeStruct((OWN, 1, WIDTH), F3...  72.5 us
    unnamed x1, local copies, waits for them, and re-layouts  2.04 us

profile of v2, /device:TPU:8, one launch (start us, length us, event | category | flops | bytes accessed | tf_op | source)
XLA Modules:
  0.0 74.5 jit_solution(276220397078092887)
XLA Ops:
  0.0 72.5 %shard_map.127 = f32[135,1,768]{2,1,0:T(1,128)} custom-call(bf16[1,12,1536]{2,1,0:T(8,128)(2,1)} %enc.1, s32[1,12]{1,0:T(1,128)} %vis.1, s32[8640]{0:T(1024)} %owner.1, bf16[1536]{0:T(1024)(128)(2,1)} %enc_g.1, bf16[768]{0:T(1024)(128)(2,1)} %mask_t.1, bf16[768]{0:T(1024)(128)(2,1)} %attn_g.1, bf16[768]{0:T(1024)(128)(2,1)} %mlp_g.1, ...), custom_call_target="tpu_custom_call" | custom-call | flops 6000000000 | bytes 5000000 | tf_op jit(solution)/shard_map/pallas_call | solution.py:653
  72.5 2.0 %copy.15 = f32[1,135,768]{2,0,1:T(1,128)} copy(f32[1,135,768]{2,0,1:T(1,128)} %bitcast.4) | data formatting | bytes 829440

commit v3 on v2

--- a/solution.py
+++ b/solution.py
@@ -92,8 +92,7 @@
     E2, W2, OA, OB, U2, D2, own2, encf, vrow, P1, P2, R1, R2, GQ, GE, GK1, GK2, IDG,
     rankf, KT, VT, XC, XE, PB, RX, YX, SC, QB, ACC, MX, LS, STREAM, MID,
     loc_sem, ws, wr, os_, or_, os2, or2, fs, fr, p1s, p1r, p2s, p2r,
-    ids_ps, ids_pr, ids_ms, ids_mr, q_ps, q_pr, q_ms, q_mr, e_ps, e_pr, e_ms, e_mr,
-    k1_ps, k1_pr, k1_ms, k1_mr, k2_ps, k2_pr, k2_ms, k2_mr,
+    ids_s, ids_r, q_s, q_r, e_s, e_r, k1_s, k1_r, k2_s, k2_r,
     xcs, xcr, xes, xer, rss, rsr, ags, agr,
 ):
     s = lax.axis_index("section")
@@ -128,7 +127,7 @@
     class Group:
         def __init__(self, copy, n, slot, ref, recv):
             self.copy, self.n, self.slot, self.ref, self.sem = copy, n, slot, ref, recv
-            self.waited = False
+            self.waited = self.gone = False
             groups.append(self)
             ring(n)(lambda k: copy(k).start())
 
@@ -141,7 +140,9 @@
             ring(self.n)(self.wait_one)
 
         def left(self):
-            ring(self.n)(lambda k: self.copy(k).wait_send())
+            if not self.gone:
+                self.gone = True
+                ring(self.n)(lambda k: self.copy(k).wait_send())
 
     class Single:
         def __init__(self, copy):
@@ -156,50 +157,6 @@
 
         def left(self):
             self.copy.wait_send()
-
-    class Ring:
-        def __init__(self, ref, me, device, plus, sems):
-            self.ref, self.me, self.device, self.plus, self.minus = ref, me, device, plus, 7 - plus
-            self.ps, self.pr, self.ms, self.mr = sems
-            self.waited = False
-            groups.append(self)
-            self.up(1).start()
-            self.down(1).start()
-
-        def up(self, t):
-            block = self.ref.at[(self.me + 9 - t) % 8]
-            return remote(block, block, self.ps.at[t], self.pr.at[t], self.device(1))
-
-        def down(self, t):
-            block = self.ref.at[(self.me + t - 1) % 8]
-            return remote(block, block, self.ms.at[t], self.mr.at[t], self.device(7))
-
-        def hop(self, t):
-            def receive(block, sem):
-                there = self.ref.at[block]
-                remote(there, there, sem.at[t], sem.at[t], partner).wait_recv()
-
-            def guard(condition, f):
-                if isinstance(t, int):
-                    if condition:
-                        f()
-                else:
-                    pl.when(condition)(f)
-
-            guard(t <= self.plus, lambda: receive((self.me + 8 - t) % 8, self.pr))
-            guard(t < self.plus, lambda: self.up(t + 1).start())
-            guard(t <= self.minus, lambda: receive((self.me + t) % 8, self.mr))
-            guard(t < self.minus, lambda: self.down(t + 1).start())
-            if isinstance(t, int) and t == 4:
-                self.waited = True
-
-        def wait(self):
-            for t in range(1, 5):
-                self.hop(t)
-
-        def left(self):
-            ring(self.plus + 1)(lambda t: self.up(t).wait_send())
-            ring(self.minus + 1)(lambda t: self.down(t).wait_send())
 
     class Local:
         def __init__(self, copy):
@@ -432,34 +389,26 @@
 
         return Group(copy, n, source, ref, recv)
 
-    r_ids = Ring(IDG, y, ydev, 4, (ids_ps, ids_pr, ids_ms, ids_mr))
-    r_q = Ring(GQ, y, ydev, 4, (q_ps, q_pr, q_ms, q_mr))
-    r_e = Ring(GE, z, zdev, 4, (e_ps, e_pr, e_ms, e_mr))
+    c_q = over(8, GQ, y, from_y, q_s, q_r, ydev)
+    c_ids = over(8, IDG, y, from_y, ids_s, ids_r, ydev)
+    c_e = over(8, GE, z, from_z, e_s, e_r, zdev)
 
     def build_some(low, high):
         lax.fori_loop(low, high, lambda c, x: (build(c), x)[1], 0)
 
-    def hop_early(t):
-        r_ids.hop(t)
-        r_q.hop(t)
-        r_e.hop(t)
-
-    build_some(6, 9)
-    hop_early(1)
     local[4].wait()
     local[5].wait()
     g_oa.wait()
     g_ob.wait()
     forward_a = Single(remote(OA.at[s], OA.at[s], fs.at[0], fr.at[0], partner))
     forward_b = Single(remote(OB.at[s], OB.at[s], fs.at[1], fr.at[1], partner))
-    build_some(9, 12)
-    hop_early(2)
-    build_some(12, 15)
-    hop_early(3)
-    r_k1 = Ring(GK1, y, ydev, 3, (k1_ps, k1_pr, k1_ms, k1_mr))
-    r_k2 = Ring(GK2, z, zdev, 3, (k2_ps, k2_pr, k2_ms, k2_mr))
-    build_some(15, 17)
-    hop_early(4)
+    build_some(6, 13)
+    c_q.left()
+    c_k1 = over(8, GK1, y, from_y, k1_s, k1_r, ydev)
+    c_e.left()
+    c_k2 = over(8, GK2, z, from_z, k2_s, k2_r, zdev)
+    build_some(13, 17)
+    c_ids.wait()
 
     ids = IDG[...].reshape(64, 128)
     lane_i = fiota((64, 128), 1)
@@ -511,6 +460,7 @@
         both = one + pltpu.roll(two, LOCAL, 1)
         return jnp.where(iota((ROWS, 256), 1) < LOCAL, both[:, 0:256], 0.0)
 
+    c_q.wait()
     q_vis = choose(row_yz, GQ[...].reshape(384, 384))
     queries = jnp.where(is_vis, q_vis, q_masked).astype(BF16).astype(F32) * (HD ** -0.5)
     lane_q = iota((ROWS, 256), 1)
@@ -520,6 +470,7 @@
             keep, queries, jnp.where(lane_q == LOCAL, 1.0, 0.0)
         ).astype(BF16)
 
+    c_e.wait()
     XE[m] = choose(row_zy, GE[...].reshape(384, 384)).astype(BF16)
 
     c_xe = over(4, XE, m, from_x, xes, xer, xdev)
@@ -541,16 +492,15 @@
         ACC[...] = ACC[...] * jnp.concatenate([factor, factor], axis=1) + product(weights_.astype(BF16))
 
     def masked(c, x):
-        r_k1.hop(c + 1)
-        r_k2.hop(c + 1)
         start = pl.multiple_of(c * CHUNK, 128)
         scores = nn(QB[...], KT[:, pl.ds(start, CHUNK)])
         absorb(scores, CHUNK, lambda w: nt(w, VT[:, pl.ds(start, CHUNK)]))
         return x
 
     lax.fori_loop(0, KEYS // CHUNK, masked, 0)
-    r_k1.waited = r_k2.waited = True
-
+
+    c_k1.wait()
+    c_k2.wait()
     q_only = jnp.where(iota((3 * ROWS, 256), 1) < LOCAL, QB[...].astype(F32), 0.0).astype(BF16)
 
     seen_rows = jnp.concatenate([GK1[...].reshape(384, 384), GK2[...].reshape(384, 384)], axis=0)
@@ -649,7 +599,7 @@
         V((8, 128), F32), V((3 * ROWS, 256), BF16), V((3 * ROWS, 256), F32),
         V((3 * ROWS, 128), F32), V((3 * ROWS, 128), F32), V((ROWS, WIDTH), F32), V((ROWS, WIDTH), F32),
         dma((6,)), dma((4,)), dma((4,)), dma((4,)), dma((4,)), dma((4,)), dma((4,)), dma((2,)), dma((2,)),
-    ] + [dma((8,))] * 4 + [dma((5,))] * 20 + [dma((4,))] * 8
+    ] + [dma((8,))] * 14 + [dma((4,))] * 8
     decoded = pl.pallas_call(
         kernel,
         out_shape=jax.ShapeDtypeStruct((OWN, 1, WIDTH), F32),

time: 74.8 us -> 69.4 us (0.928)
  Pallas kernels: 72.5 us -> 67.2 us
    pallas_call x1, Pallas kernels: 72.5 us -> 67.2 us  [shards(): pl.pallas_call(kernel, out_shape=jax.ShapeDtypeStruct((OWN, 1, WIDTH), F3...]
where the time goes in v3:
time: 69.4 us; the launch traced here: 69.3 us
  Pallas kernels  67.2 us (97%)
  local copies, waits for them, and re-layouts  2.04 us (3%)
    pallas_call x1, Pallas kernels, shards(): pl.pallas_call(kernel, out_shape=jax.ShapeDtypeStruct((OWN, 1, WIDTH), F3...  67.2 us
    unnamed x1, local copies, waits for them, and re-layouts  2.04 us

profile of v3, /device:TPU:8, one launch (start us, length us, event | category | flops | bytes accessed | tf_op | source)
XLA Modules:
  0.0 69.3 jit_solution(5861189727589351462)
XLA Ops:
  0.0 67.2 %shard_map.127 = f32[135,1,768]{2,1,0:T(1,128)} custom-call(bf16[1,12,1536]{2,1,0:T(8,128)(2,1)} %enc.1, s32[1,12]{1,0:T(1,128)} %vis.1, s32[8640]{0:T(1024)} %owner.1, bf16[1536]{0:T(1024)(128)(2,1)} %enc_g.1, bf16[768]{0:T(1024)(128)(2,1)} %mask_t.1, bf16[768]{0:T(1024)(128)(2,1)} %attn_g.1, bf16[768]{0:T(1024)(128)(2,1)} %mlp_g.1, ...), custom_call_target="tpu_custom_call" | custom-call | flops 6000000000 | bytes 5000000 | tf_op jit(solution)/shard_map/pallas_call | solution.py:603
  67.2 2.0 %copy.15 = f32[1,135,768]{2,0,1:T(1,128)} copy(f32[1,135,768]{2,0,1:T(1,128)} %bitcast.4) | data formatting | bytes 829440

commit v4 on v3

--- a/solution.py
+++ b/solution.py
@@ -116,9 +116,17 @@
             src_ref=src, dst_ref=dst, send_sem=send, recv_sem=recv, device_id=device, device_id_type=MESH
         )
 
-    def ring(n, first=1):
+    def ring(n):
         def run(f):
-            lax.fori_loop(first, n, lambda k, c: (f(k), c)[1], 0)
+            lax.fori_loop(1, n, lambda k, c: (f(k), c)[1], 0)
+
+        return run
+
+    def far_first(n):
+        def run(f):
+            lax.fori_loop(
+                0, n - 1, lambda j, c: (f(n // 2 + ((j + 1) // 2) * (1 - 2 * (j % 2))), c)[1], 0
+            )
 
         return run
 
@@ -129,7 +137,7 @@
             self.copy, self.n, self.slot, self.ref, self.sem = copy, n, slot, ref, recv
             self.waited = self.gone = False
             groups.append(self)
-            ring(n)(lambda k: copy(k).start())
+            far_first(n)(lambda k: copy(k).start())
 
         def wait_one(self, k):
             there = self.ref.at[self.slot(k)]
@@ -191,10 +199,12 @@
         return pltpu.make_async_copy(ref_in, ref_out.at[s], loc_sem.at[i])
 
     barrier = pltpu.get_barrier_semaphore()
-    pl.semaphore_signal(barrier, inc=1, device_id=partner, device_id_type=MESH)
-    ring(8)(lambda k: pl.semaphore_signal(barrier, inc=1, device_id=zdev(k), device_id_type=MESH))
-    ring(8)(lambda k: pl.semaphore_signal(barrier, inc=1, device_id=ydev(k), device_id_type=MESH))
-    ring(4)(lambda k: pl.semaphore_signal(barrier, inc=1, device_id=xdev(k), device_id_type=MESH))
+    def greet(device):
+        pl.semaphore_signal(barrier, inc=1, device_id=device, device_id_type=MESH)
+
+    far_first(8)(lambda k: (greet(zdev(k)), greet(ydev(k))))
+    far_first(4)(lambda k: greet(xdev(k)))
+    greet(partner)
 
     local = [
         Local(copy)
@@ -389,8 +399,8 @@
 
         return Group(copy, n, source, ref, recv)
 
+    c_ids = over(8, IDG, y, from_y, ids_s, ids_r, ydev)
     c_q = over(8, GQ, y, from_y, q_s, q_r, ydev)
-    c_ids = over(8, IDG, y, from_y, ids_s, ids_r, ydev)
     c_e = over(8, GE, z, from_z, e_s, e_r, zdev)
 
     def build_some(low, high):
@@ -403,9 +413,7 @@
     forward_a = Single(remote(OA.at[s], OA.at[s], fs.at[0], fr.at[0], partner))
     forward_b = Single(remote(OB.at[s], OB.at[s], fs.at[1], fr.at[1], partner))
     build_some(6, 13)
-    c_q.left()
     c_k1 = over(8, GK1, y, from_y, k1_s, k1_r, ydev)
-    c_e.left()
     c_k2 = over(8, GK2, z, from_z, k2_s, k2_r, zdev)
     build_some(13, 17)
     c_ids.wait()

time: 69.4 us -> 67.6 us (0.974)
  Pallas kernels: 67.2 us -> 65.3 us
    pallas_call x1, Pallas kernels: 67.2 us -> 65.3 us  [shards(): pl.pallas_call(kernel, out_shape=jax.ShapeDtypeStruct((OWN, 1, WIDTH), F3...]
where the time goes in v4:
time: 67.6 us; the launch traced here: 67.4 us
  Pallas kernels  65.3 us (97%)
  local copies, waits for them, and re-layouts  2.04 us (3%)
    pallas_call x1, Pallas kernels, shards(): pl.pallas_call(kernel, out_shape=jax.ShapeDtypeStruct((OWN, 1, WIDTH), F3...  65.3 us
    unnamed x1, local copies, waits for them, and re-layouts  2.04 us

profile of v4, /device:TPU:8, one launch (start us, length us, event | category | flops | bytes accessed | tf_op | source)
XLA Modules:
  0.0 67.4 jit_solution(2286466666608094287)
XLA Ops:
  0.0 65.3 %shard_map.127 = f32[135,1,768]{2,1,0:T(1,128)} custom-call(bf16[1,12,1536]{2,1,0:T(8,128)(2,1)} %enc.1, s32[1,12]{1,0:T(1,128)} %vis.1, s32[8640]{0:T(1024)} %owner.1, bf16[1536]{0:T(1024)(128)(2,1)} %enc_g.1, bf16[768]{0:T(1024)(128)(2,1)} %mask_t.1, bf16[768]{0:T(1024)(128)(2,1)} %attn_g.1, bf16[768]{0:T(1024)(128)(2,1)} %mlp_g.1, ...), custom_call_target="tpu_custom_call" | custom-call | flops 6000000000 | bytes 5000000 | tf_op jit(solution)/shard_map/pallas_call | solution.py:611
  65.4 2.0 %copy.15 = f32[1,135,768]{2,0,1:T(1,128)} copy(f32[1,135,768]{2,0,1:T(1,128)} %bitcast.4) | data formatting | bytes 829440

commit v5 on v4

--- a/solution.py
+++ b/solution.py
@@ -87,9 +87,9 @@
 
 
 def kernel(
-    enc, vis, owner, enc_g, mask_t, attn_g, mlp_g, ct3, embed_w, qkv_w, out_w, up_w, down_w,
+    enc_h, vis, owner, enc_gh, mask_h, attn_h, mlp_h, ct3_h, embed_w, qkv_w, out_w, up_w, down_w,
     result,
-    E2, W2, OA, OB, U2, D2, own2, encf, vrow, P1, P2, R1, R2, GQ, GE, GK1, GK2, IDG,
+    E2, W2, OA, OB, U2, D2, own2, enc, enc_g, mask_t, attn_g, mlp_g, ct3, encf, vrow, P1, P2, R1, R2, GQ, GE, GK1, GK2, IDG,
     rankf, KT, VT, XC, XE, PB, RX, YX, SC, QB, ACC, MX, LS, STREAM, MID,
     loc_sem, ws, wr, os_, or_, os2, or2, fs, fr, p1s, p1r, p2s, p2r,
     ids_s, ids_r, q_s, q_r, e_s, e_r, k1_s, k1_r, k2_s, k2_r,
@@ -206,6 +206,14 @@
     far_first(4)(lambda k: greet(xdev(k)))
     greet(partner)
 
+    small = [
+        pltpu.make_async_copy(src, dst, loc_sem.at[6 + i])
+        for i, (src, dst) in enumerate(
+            ((enc_h, enc), (ct3_h, ct3), (enc_gh, enc_g), (mask_h, mask_t), (attn_h, attn_g), (mlp_h, mlp_g))
+        )
+    ]
+    for copy in small:
+        copy.start()
     local = [
         Local(copy)
         for copy in (
@@ -215,6 +223,8 @@
         )
     ]
 
+    for copy in small:
+        copy.wait()
     mask_row = mask_t[...].astype(F32).reshape(1, WIDTH)
     attn_gain = attn_g[...].astype(F32).reshape(1, WIDTH)
     mlp_gain = mlp_g[...].astype(F32).reshape(1, WIDTH)
@@ -579,8 +589,8 @@
     c_ag.wait()
     for half in range(2):
         cols = slice(half * 384, (half + 1) * 384)
-        result[0:80, :, cols] = (MID[0:80, cols] + YX[half].astype(F32))[:, None, :]
-        result[80:OWN, :, cols] = (MID[80:OWN, cols] + YX[2 + half].astype(F32)[16:71])[:, None, :]
+        result[0:80, cols] = MID[0:80, cols] + YX[half].astype(F32)
+        result[80:OWN, cols] = MID[80:OWN, cols] + YX[2 + half].astype(F32)[16:71]
 
     finish()
 
@@ -597,6 +607,8 @@
     scratch = [
         V((2, 768, 768), BF16), V((2, 576, 384), BF16), V((2, 4, 128, 384), BF16), V((2, 4, 64, 384), BF16),
         V((2, 384, 768), BF16), V((2, 768, 384), BF16), V((72, 128), jnp.int32),
+        V((1, VIS_DEV, ENC), BF16), V((ENC,), BF16), V((WIDTH,), BF16), V((WIDTH,), BF16), V((WIDTH,), BF16),
+        V((192, WIDTH), BF16),
         V((16, ENC), F32), V((8, 128), F32), V((16, 384), BF16), V((16, 384), BF16),
         V((8, 16, 384), BF16), V((8, 16, 384), BF16),
         V((8, 48, 384), BF16), V((8, 48, 384), BF16), V((8, 48, 384), BF16), V((8, 48, 384), BF16),
@@ -606,12 +618,12 @@
         V((2, ROWS, 384), BF16), V((4, 80, 384), BF16), V((4, 80, 384), BF16),
         V((8, 128), F32), V((3 * ROWS, 256), BF16), V((3 * ROWS, 256), F32),
         V((3 * ROWS, 128), F32), V((3 * ROWS, 128), F32), V((ROWS, WIDTH), F32), V((ROWS, WIDTH), F32),
-        dma((6,)), dma((4,)), dma((4,)), dma((4,)), dma((4,)), dma((4,)), dma((4,)), dma((2,)), dma((2,)),
+        dma((12,)), dma((4,)), dma((4,)), dma((4,)), dma((4,)), dma((4,)), dma((4,)), dma((2,)), dma((2,)),
     ] + [dma((8,))] * 14 + [dma((4,))] * 8
     decoded = pl.pallas_call(
         kernel,
-        out_shape=jax.ShapeDtypeStruct((OWN, 1, WIDTH), F32),
-        in_specs=[vm] * 8 + [hbm, hbm, hbm, hbm, hbm],
+        out_shape=jax.ShapeDtypeStruct((OWN, WIDTH), F32),
+        in_specs=[hbm, vm, vm] + [hbm] * 5 + [hbm, hbm, hbm, hbm, hbm],
         out_specs=vm,
         scratch_shapes=scratch,
         compiler_params=pltpu.CompilerParams(
@@ -622,7 +634,7 @@
         enc_rows, vis_index, owner_of, enc_gain, mask_token, attn_gain, mlp_gain, jnp.asarray(code_table()),
         embed_weight, qkv_t, out_weight, up_weight, down_weight,
     )
-    return jnp.transpose(decoded, (1, 0, 2))
+    return decoded[None]
 
 
 def solution(mesh):

time: 67.6 us -> 67.5 us (level)
  the two profiles are of different devices: /device:TPU:8 before, /device:TPU:2 now
where the time goes in v5:
time: 67.5 us; the launch traced here: 67.3 us
  Pallas kernels  65.1 us (96%)
  local copies, waits for them, and re-layouts  2.18 us (3%)
    pallas_call x1, Pallas kernels, shards(): pl.pallas_call(kernel, out_shape=jax.ShapeDtypeStruct((OWN, WIDTH), F32),...  65.1 us
    broadcast_in_dim x1, local copies, waits for them, and re-layouts, shards(): return decoded[None]  2.18 us

profile of v5, /device:TPU:2, one launch (start us, length us, event | category | flops | bytes accessed | tf_op | source)
XLA Modules:
  0.0 67.3 jit_solution(5430762218275534325)
XLA Ops:
  0.0 65.1 %shard_map.127 = f32[135,768]{1,0:T(8,128)} custom-call(bf16[1,12,1536]{2,1,0:T(8,128)(2,1)} %enc_h.1, s32[1,12]{1,0:T(1,128)} %vis.1, s32[8640]{0:T(1024)} %owner.1, bf16[1536]{0:T(1024)(128)(2,1)} %enc_gh.1, bf16[768]{0:T(1024)(128)(2,1)} %mask_h.1, bf16[768]{0:T(1024)(128)(2,1)} %attn_h.1, bf16[768]{0:T(1024)(128)(2,1)} %mlp_h.1, ...), custom_call_target="tpu_custom_call" | custom-call | flops 6000000000 | bytes 5000000 | tf_op jit(solution)/shard_map/pallas_call | solution.py:623
  65.1 2.2 %copy.14 = f32[1,135,768]{2,0,1:T(1,128)} copy(f32[1,135,768]{2,1,0:T(8,128)} %bitcast.4) | data formatting | bytes 829440 | tf_op jit(solution)/shard_map/broadcast_in_dim | solution.py:637

commit v6 on v5

--- a/solution.py
+++ b/solution.py
@@ -133,11 +133,12 @@
     groups = []
 
     class Group:
-        def __init__(self, copy, n, slot, ref, recv):
+        def __init__(self, copy, n, slot, ref, recv, now=True):
             self.copy, self.n, self.slot, self.ref, self.sem = copy, n, slot, ref, recv
             self.waited = self.gone = False
             groups.append(self)
-            far_first(n)(lambda k: copy(k).start())
+            if now:
+                far_first(n)(lambda k: copy(k).start())
 
         def wait_one(self, k):
             there = self.ref.at[self.slot(k)]
@@ -388,7 +389,6 @@
     lax.fori_loop(0, 6, lambda c, x: (build(c), x)[1], 0)
 
     g_p1.wait()
-    g_p2.wait()
     col = fiota((112, 1), 0)
     small = jnp.where(col < 48, col, col - 48)
     src = jnp.floor((small + 0.5) * (1.0 / 6.0))
@@ -396,12 +396,9 @@
     src = jnp.where(col < 96, src, jnp.where(col < 104, 16.0 * (col - 96) + 12, 16.0 * (col - 104) + 13))
     chooser = select(col, src, 128)
     got1 = nn(chooser, R1[...].reshape(128, 384))
-    got2 = nn(chooser[0:96], R2[...].reshape(128, 384))
     GQ[y] = got1[0:48].astype(BF16)
     GK1[y] = got1[48:96].astype(BF16)
     IDG[y] = 128.0 * got1[96:104, 0:128] + got1[104:112, 0:128]
-    GE[z] = got2[0:48].astype(BF16)
-    GK2[z] = got2[48:96].astype(BF16)
 
     def over(n, ref, slot, source, send, recv, device):
         def copy(k):
@@ -411,6 +408,10 @@
 
     c_ids = over(8, IDG, y, from_y, ids_s, ids_r, ydev)
     c_q = over(8, GQ, y, from_y, q_s, q_r, ydev)
+    g_p2.wait()
+    got2 = nn(chooser[0:96], R2[...].reshape(128, 384))
+    GE[z] = got2[0:48].astype(BF16)
+    GK2[z] = got2[48:96].astype(BF16)
     c_e = over(8, GE, z, from_z, e_s, e_r, zdev)
 
     def build_some(low, high):
@@ -570,16 +571,20 @@
     mlp_in = (norm(MID[...]) * mlp_gain).astype(BF16)
     raised = nn(mlp_in[:, 0:384], U2[0]) + nn(mlp_in[:, 384:768], U2[1])
     hidden = (0.5 * raised * (1.0 + lax.erf(raised * np.float32(np.sqrt(0.5))))).astype(BF16)
+    def quadrant(q):
+        return PB.at[q % 2, pl.ds(pl.multiple_of((q // 2) * 64, 16), 80)]
+
+    def rs_copy(k):
+        return remote(quadrant((m + k) % 4), RX.at[m], rss.at[k], rsr.at[k], xdev(k))
+
+    c_rs = Group(rs_copy, 4, from_x, RX, rsr, now=False)
     for half in range(2):
         PB[half] = nn(hidden, D2[half]).astype(BF16)
 
-    def quadrant(q):
-        return PB.at[q % 2, pl.ds(pl.multiple_of((q // 2) * 64, 16), 80)]
-
-    def rs_copy(k):
-        return remote(quadrant((m + k) % 4), RX.at[m], rss.at[k], rsr.at[k], xdev(k))
-
-    c_rs = Group(rs_copy, 4, from_x, RX, rsr)
+        def send(k, half=half):
+            pl.when((m + k) % 2 == half)(lambda: rs_copy(k).start())
+
+        far_first(4)(send)
     RX[m] = PB[m % 2, pl.ds(pl.multiple_of((m // 2) * 64, 16), 80), :]
     c_rs.wait()
     YX[m] = (

time: 67.5 us -> 67.8 us (level)
  the two profiles are of different devices: /device:TPU:2 before, /device:TPU:8 now
where the time goes in v6:
time: 67.8 us; the launch traced here: 67.6 us
  Pallas kernels  65.4 us (96%)
  local copies, waits for them, and re-layouts  2.18 us (3%)
    pallas_call x1, Pallas kernels, shards(): pl.pallas_call(kernel, out_shape=jax.ShapeDtypeStruct((OWN, WIDTH), F32),...  65.4 us
    broadcast_in_dim x1, local copies, waits for them, and re-layouts, shards(): return decoded[None]  2.18 us

profile of v6, /device:TPU:8, one launch (start us, length us, event | category | flops | bytes accessed | tf_op | source)
XLA Modules:
  0.0 67.6 jit_solution(13515541851235097033)
XLA Ops:
  0.0 65.4 %shard_map.127 = f32[135,768]{1,0:T(8,128)} custom-call(bf16[1,12,1536]{2,1,0:T(8,128)(2,1)} %enc_h.1, s32[1,12]{1,0:T(1,128)} %vis.1, s32[8640]{0:T(1024)} %owner.1, bf16[1536]{0:T(1024)(128)(2,1)} %enc_gh.1, bf16[768]{0:T(1024)(128)(2,1)} %mask_h.1, bf16[768]{0:T(1024)(128)(2,1)} %attn_h.1, bf16[768]{0:T(1024)(128)(2,1)} %mlp_h.1, ...), custom_call_target="tpu_custom_call" | custom-call | flops 6000000000 | bytes 5000000 | tf_op jit(solution)/shard_map/pallas_call | solution.py:628
  65.4 2.2 %copy.14 = f32[1,135,768]{2,0,1:T(1,128)} copy(f32[1,135,768]{2,1,0:T(8,128)} %bitcast.4) | data formatting | bytes 829440 | tf_op jit(solution)/shard_map/broadcast_in_dim | solution.py:642
